TPU v7x, 32 devices: a whole 2x2x4 slice. The times are simulated.
32 devices in a mesh: ctx: 16 (over z, y, x), tp: 2 (over core).
Axes of the slice: x: 2, y: 2, z: 4, core: 2. Of those that a mesh axis runs over, the one named last changes fastest.
Arguments:
- inputs: bfloat16 [3, 4096, 8192], P(None, 'ctx', 'tp'), may hold values from -6 to 6
- cotangent: bfloat16 [4096, 8192], P('ctx', 'tp'), may hold values from -140 to 140
- short_filter: float32 [3, 7, 8192], P(None, None, 'tp'), may hold values from -2 to 2
- residue: float32 [16, 8192], P(None, 'tp'), may hold values from -0.22 to 0.22
- decay_rate: float32 [16, 8192], P(None, 'tp'), may hold values from 2.4414063e-05 to 0.04
Outputs:
- grad_inputs: bfloat16 [3, 4096, 8192], P(None, 'ctx', 'tp')
- grad_short: float32 [3, 7, 8192], P(None, None, 'tp')
All inputs are finite; a program needn't handle non-finite values.
Results may differ from a plain program's by a relative error of at most 0.0057.
Values may be sent and summed in bfloat16 or wider, within the bound.
A program may use at most 320 MiB of HBM per device.

v0:
```python
import math

import jax
import jax.numpy as jnp
import numpy as np
from jax import lax
from jax.experimental import pallas as pl
from jax.experimental.pallas import tpu as pltpu
from jax.sharding import PartitionSpec as P

LANES = 128
RIM = 8
VMEM_LIMIT = 48 * 1024 * 1024


def passed_along(shard, axis, by):
    length = lax.axis_size(axis)
    pairs = [(i, i + by) for i in range(length) if 0 <= i + by < length]
    return lax.ppermute(shard, axis, pairs)


def spectral_table(rows):
    frame = 2 * rows
    freq = np.arange(rows)[:, None]
    pos = np.arange(rows)[None, :]
    angles = (freq * pos % frame) * (2.0 * math.pi / frame)
    lower = -np.sin(angles)
    lower[0] = 1.0 - 2.0 * (np.arange(rows) % 2)
    return np.concatenate([np.cos(angles), lower], axis=0).astype(np.float32)


def split_table(table):
    high = table.astype(jnp.bfloat16)
    low = (table - high.astype(np.float32)).astype(jnp.bfloat16)
    return high, low


def mm(a, b):
    return jnp.dot(a, b, preferred_element_type=jnp.float32)


def row_ids():
    return lax.broadcasted_iota(jnp.int32, (8, LANES), 0).astype(jnp.float32)


def filter_kernel(res_ref, rate_ref, high_ref, low_ref, spec_ref, taps):
    modes, width = res_ref.shape
    rows = taps.shape[0]
    ids = row_ids()

    @pl.loop(0, width // LANES)
    def _(chunk):
        lanes = pl.ds(pl.multiple_of(chunk * LANES, LANES), LANES)
        terms = []
        steps = []
        for n in range(modes):
            rate = jnp.broadcast_to(rate_ref[n : n + 1, lanes], (8, LANES))
            terms.append(res_ref[n : n + 1, lanes] * jnp.exp(-rate * ids))
            steps.append(jnp.exp(-8.0 * rate))

        def body(block, terms):
            total = list(terms)
            while len(total) > 1:
                total = [total[i] + total[i + 1] for i in range(0, len(total) - 1, 2)] + (
                    [total[-1]] if len(total) % 2 else []
                )
            taps[pl.ds(pl.multiple_of(block * 8, 8), 8), lanes] = total[0]
            return tuple(t * s for t, s in zip(terms, steps))

        lax.fori_loop(0, rows // 8, body, tuple(terms), unroll=4)

    whole = taps[...]
    main = whole.astype(jnp.bfloat16)
    rest = (whole - main.astype(jnp.float32)).astype(jnp.bfloat16)
    spec = mm(high_ref[...], main) + (mm(low_ref[...], main) + mm(high_ref[...], rest))
    index = lax.broadcasted_iota(jnp.int32, spec.shape, 0)
    edge = jnp.logical_or(index == 0, index == rows)
    spec_ref[...] = spec * jnp.where(edge, 0.5 / rows, 1.0 / rows)


def fill_extended(ext, in_ref, rim_ref, lanes):
    rows = in_ref.shape[1]
    for i in range(3):
        ext[i, 0:RIM, :] = rim_ref[i, :, lanes]
        ext[i, RIM : RIM + rows, :] = in_ref[i, :, lanes].astype(jnp.float32)


def mix_kernel(
    in_ref, rim_ref, cot_ref, short_ref, rate_ref,
    gated_ref, grad_ref, key_ref, value_ref, state_ref, ext, rowed,
):
    rows, width = cot_ref.shape
    modes = rate_ref.shape[0]
    taps = short_ref.shape[1]
    part = 32
    ids = row_ids()

    @pl.loop(0, width // LANES)
    def _(chunk):
        lanes = pl.ds(pl.multiple_of(chunk * LANES, LANES), LANES)
        fill_extended(ext, in_ref, rim_ref, lanes)
        for first in range(0, rows, part):
            mixed = []
            for i in range(3):
                total = None
                for j in range(taps):
                    term = short_ref[i, j : j + 1, lanes] * ext[i, first + RIM - j : first + RIM - j + part, :]
                    total = term if total is None else total + term
                mixed.append(total)
            here = slice(first, first + part)
            gated_ref[here, lanes] = (mixed[1] * mixed[2]).astype(jnp.bfloat16)
            grad_ref[here, lanes] = (cot_ref[here, lanes].astype(jnp.float32) * mixed[0]).astype(jnp.bfloat16)
            key_ref[here, lanes] = mixed[1].astype(jnp.bfloat16)
            value_ref[here, lanes] = mixed[2].astype(jnp.bfloat16)

        steps = [
            jnp.exp(-8.0 * jnp.broadcast_to(rate_ref[n : n + 1, lanes], (8, LANES)))
            for n in range(modes)
        ]

        def body(block, carry):
            ends, starts = carry
            up = pl.multiple_of(block * 16, 16)
            down = pl.multiple_of(rows - 16 - block * 16, 16)
            ahead = gated_ref[pl.ds(up, 16), lanes].astype(jnp.float32)
            behind = grad_ref[pl.ds(down, 16), lanes].astype(jnp.float32)
            ends = [e * s + ahead[0:8] for e, s in zip(ends, steps)]
            starts = [e * s + behind[8:16] for e, s in zip(starts, steps)]
            ends = [e * s + ahead[8:16] for e, s in zip(ends, steps)]
            starts = [e * s + behind[0:8] for e, s in zip(starts, steps)]
            return tuple(ends), tuple(starts)

        zero = tuple(jnp.zeros((8, LANES), jnp.float32) for _ in range(modes))
        ends, starts = lax.fori_loop(0, rows // 16, body, (zero, zero), unroll=2)
        for n in range(modes):
            rate = jnp.broadcast_to(rate_ref[n : n + 1, lanes], (8, LANES))
            rowed[n : n + 1, :] = jnp.sum(ends[n] * jnp.exp(-rate * (7.0 - ids)), axis=0, keepdims=True)
            rowed[modes + n : modes + n + 1, :] = jnp.sum(
                starts[n] * jnp.exp(-rate * ids), axis=0, keepdims=True
            )
        state_ref[0, :, lanes] = rowed[0:modes, :].astype(jnp.bfloat16)
        state_ref[1, :, lanes] = rowed[modes : 2 * modes, :].astype(jnp.bfloat16)


def local_kernel(gated_ref, grad_ref, spec_ref, high_ref, low_ref, hight_ref, lowt_ref, fwd_ref, back_ref):
    rows = gated_ref.shape[0]
    real = spec_ref[0:rows, :]
    lower = spec_ref[rows : 2 * rows, :]
    first = lax.broadcasted_iota(jnp.int32, real.shape, 0) == 0
    imag = jnp.where(first, 0.0, lower)
    other = jnp.where(first, lower, real)

    def convolved(signal, sign, out_ref):
        seen = mm(high_ref[...], signal) + mm(low_ref[...], signal)
        a = seen[0:rows, :]
        b = seen[rows : 2 * rows, :]
        imag_s = imag * sign
        top = (a * real - b * imag_s).astype(jnp.bfloat16)
        bottom = (a * imag_s + b * other).astype(jnp.bfloat16)
        both = jnp.concatenate([top, bottom], axis=0)
        out_ref[...] = mm(hight_ref[...], both) + mm(lowt_ref[...], both)

    convolved(gated_ref[...], 1.0, fwd_ref)
    convolved(grad_ref[...], -1.0, back_ref)


def scan_kernel(states_ref, step_ref, out_ref):
    count = states_ref.shape[0]
    step = step_ref[...]
    zero = jnp.zeros(step.shape, jnp.float32)

    def up(j, carry):
        out_ref[j, 0, :, :] = carry.astype(jnp.bfloat16)
        return carry * step + states_ref[j, 0, :, :].astype(jnp.float32)

    lax.fori_loop(0, count, up, zero)

    def down(i, carry):
        j = count - 1 - i
        out_ref[j, 1, :, :] = carry.astype(jnp.bfloat16)
        return carry * step + states_ref[j, 1, :, :].astype(jnp.float32)

    lax.fori_loop(0, count, down, zero)


def apply_kernel(
    bound_ref, res_ref, rate_ref, fwd_ref, back_ref, key_ref, value_ref, cot_ref, in_ref, rim_ref,
    gm_ref, short_ref, ext, far,
):
    rows, width = cot_ref.shape
    modes = rate_ref.shape[0]
    taps = short_ref.shape[1]
    part = 32
    ids = row_ids()

    @pl.loop(0, width // LANES)
    def _(chunk):
        lanes = pl.ds(pl.multiple_of(chunk * LANES, LANES), LANES)
        fill_extended(ext, in_ref, rim_ref, lanes)
        before = bound_ref[0, :, lanes].astype(jnp.float32) * res_ref[:, lanes]
        after = bound_ref[1, :, lanes].astype(jnp.float32) * res_ref[:, lanes]
        ups = []
        downs = []
        steps = []
        for n in range(modes):
            rate = jnp.broadcast_to(rate_ref[n : n + 1, lanes], (8, LANES))
            ups.append(before[n : n + 1, :] * jnp.exp(-rate * (ids + 1.0)))
            downs.append(after[n : n + 1, :] * jnp.exp(-rate * (8.0 - ids)))
            steps.append(jnp.exp(-8.0 * rate))

        def summed(terms):
            total = list(terms)
            while len(total) > 1:
                total = [total[i] + total[i + 1] for i in range(0, len(total) - 1, 2)] + (
                    [total[-1]] if len(total) % 2 else []
                )
            return total[0]

        def body(block, carry):
            ups, downs = carry
            up = pl.ds(pl.multiple_of(block * 8, 8), 8)
            down = pl.ds(pl.multiple_of(rows - 8 - block * 8, 8), 8)
            far[0, up, :] = fwd_ref[up, lanes] + summed(ups)
            far[1, down, :] = back_ref[down, lanes] + summed(downs)
            return (
                tuple(t * s for t, s in zip(ups, steps)),
                tuple(t * s for t, s in zip(downs, steps)),
            )

        lax.fori_loop(0, rows // 8, body, (tuple(ups), tuple(downs)), unroll=2)

        sums = [[None] * taps for _ in range(3)]
        for first in range(0, rows, part):
            here = slice(first, first + part)
            mixer = far[0, here, :]
            back = far[1, here, :]
            grads = (
                cot_ref[here, lanes].astype(jnp.float32) * mixer,
                back * value_ref[here, lanes].astype(jnp.float32),
                back * key_ref[here, lanes].astype(jnp.float32),
            )
            for i in range(3):
                kept = grads[i].astype(jnp.bfloat16)
                gm_ref[i, here, lanes] = kept
                wide = kept.astype(jnp.float32)
                for j in range(taps):
                    term = wide * ext[i, first + RIM - j : first + RIM - j + part, :]
                    folded = jnp.sum(term.reshape(part // 8, 8, LANES), axis=0)
                    sums[i][j] = folded if sums[i][j] is None else sums[i][j] + folded
        for i in range(3):
            for j in range(taps):
                short_ref[i, j : j + 1, lanes] = jnp.sum(sums[i][j], axis=0, keepdims=True)


def spread_kernel(gm_ref, rim_ref, short_ref, out_ref, ext):
    rows, width = gm_ref.shape[1:]
    taps = short_ref.shape[1]
    part = 32

    @pl.loop(0, width // LANES)
    def _(chunk):
        lanes = pl.ds(pl.multiple_of(chunk * LANES, LANES), LANES)
        for i in range(3):
            ext[i, 0:rows, :] = gm_ref[i, :, lanes].astype(jnp.float32)
            ext[i, rows : rows + RIM, :] = rim_ref[i, :, lanes]
        for first in range(0, rows, part):
            for i in range(3):
                total = None
                for j in range(taps):
                    term = short_ref[i, j : j + 1, lanes] * ext[i, first + j : first + j + part, :]
                    total = term if total is None else total + term
                out_ref[i, first : first + part, lanes] = total.astype(jnp.bfloat16)


def tiled(shape, tile):
    lead = len(shape) - 1
    return pl.BlockSpec(tuple(shape[:-1]) + (tile,), lambda c: (0,) * lead + (c,))


def fixed(shape):
    return pl.BlockSpec(tuple(shape), lambda c: (0,) * len(shape))


def over_channels(kernel, operands, tables, outs, scratch, tile, flops):
    channels = operands[0].shape[-1]
    total_bytes = sum(a.size * a.dtype.itemsize for a in operands + tables)
    total_bytes += sum(math.prod(o.shape) * o.dtype.itemsize for o in outs)
    return pl.pallas_call(
        kernel,
        grid=(channels // tile,),
        in_specs=[tiled(a.shape, tile) for a in operands] + [fixed(a.shape) for a in tables],
        out_specs=[tiled(o.shape, tile) for o in outs],
        out_shape=outs,
        scratch_shapes=scratch,
        compiler_params=pltpu.CompilerParams(vmem_limit_bytes=VMEM_LIMIT),
        cost_estimate=pl.CostEstimate(flops=flops, bytes_accessed=total_bytes, transcendentals=0),
    )(*operands, *tables)


def per_device(inputs, cotangent, short_filter, residue, decay_rate):
    rows, channels = cotangent.shape
    modes = residue.shape[0]
    taps = short_filter.shape[1]
    ctx_count = lax.axis_size("ctx")
    narrow = channels // ctx_count
    tile = math.gcd(channels, 512)
    f32 = jnp.float32
    bf16 = jnp.bfloat16
    shape = jax.ShapeDtypeStruct
    high, low = split_table(spectral_table(rows))
    tables = [jnp.asarray(high), jnp.asarray(low)]
    turned = [jnp.asarray(np.ascontiguousarray(high.T)), jnp.asarray(np.ascontiguousarray(low.T))]
    ext_rows = pltpu.VMEM((3, rows + RIM, LANES), f32)

    rim = passed_along(inputs[:, rows - RIM :, :], "ctx", 1).astype(f32)
    (spec,) = over_channels(
        filter_kernel, [residue, decay_rate], tables,
        [shape((2 * rows, channels), f32)], [pltpu.VMEM((rows, tile), f32)], tile,
        6 * 2 * rows * rows * channels,
    )
    gated, grad_mixer, key_mix, value_mix, states = over_channels(
        mix_kernel, [inputs, rim, cotangent, short_filter, decay_rate], [],
        [shape((rows, channels), bf16)] * 4 + [shape((2, modes, channels), bf16)],
        [ext_rows, pltpu.VMEM((2 * modes, LANES), f32)], tile, 110 * rows * channels,
    )
    sent = states.reshape(2, modes, ctx_count, narrow).transpose(2, 0, 1, 3)
    arrived = lax.all_to_all(sent, "ctx", split_axis=0, concat_axis=0, tiled=True)
    fwd_part, back_part = over_channels(
        local_kernel, [gated, grad_mixer, spec], tables + turned,
        [shape((rows, channels), f32)] * 2, [], tile, 16 * 2 * rows * rows * channels,
    )
    first_chan = lax.axis_index("ctx") * narrow
    rate_part = lax.dynamic_slice_in_dim(decay_rate, first_chan, narrow, 1)
    bounds = pl.pallas_call(
        scan_kernel,
        out_shape=shape(arrived.shape, bf16),
        compiler_params=pltpu.CompilerParams(vmem_limit_bytes=VMEM_LIMIT),
    )(arrived, jnp.exp(-rate_part * rows))
    returned = lax.all_to_all(bounds, "ctx", split_axis=0, concat_axis=0, tiled=True)
    bound = returned.transpose(1, 2, 0, 3).reshape(2, modes, channels)
    grad_mix, short_grad = over_channels(
        apply_kernel,
        [bound, residue, decay_rate, fwd_part, back_part, key_mix, value_mix, cotangent, inputs, rim],
        [],
        [shape((3, rows, channels), bf16), shape((3, taps, channels), f32)],
        [ext_rows, pltpu.VMEM((2, rows, LANES), f32)], tile, 110 * rows * channels,
    )
    next_rim = passed_along(grad_mix[:, :RIM, :], "ctx", -1).astype(f32)
    short_sum = lax.psum(short_grad, "ctx")
    (grad_inputs,) = over_channels(
        spread_kernel, [grad_mix, next_rim, short_filter], [],
        [shape((3, rows, channels), bf16)], [ext_rows], tile, 42 * rows * channels,
    )
    squares = lax.psum(jnp.sum(short_sum * short_sum), "tp")
    clip_limit = math.sqrt(3 * channels * lax.axis_size("tp") * taps)
    factor = jnp.minimum(1.0, clip_limit / (jnp.sqrt(squares) + 1e-06))
    return (grad_inputs, short_sum * factor)


def solution(mesh):
    return jax.shard_map(
        per_device,
        mesh=mesh,
        in_specs=(
            P(None, "ctx", "tp"),
            P("ctx", "tp"),
            P(None, None, "tp"),
            P(None, "tp"),
            P(None, "tp"),
        ),
        out_specs=(P(None, "ctx", "tp"), P(None, None, "tp")),
        check_vma=False,
    )
```

profile of v0, /device:TPU:0, one launch (start us, length us, event | category | flops | bytes accessed | tf_op | source)
XLA Modules:
  0.0 260.5 jit_solution(7034862057175172006)
XLA Ops:
  8.1 4.9 %collective-permute-start = (bf16[3,8,4096]{2,1,0:T(8,128)(2,1)S(1)}, bf16[3,8,4096]{2,1,0:T(8,128)(2,1)S(1)}, u32[]{:S(2)}, u32[]{:S(2)}) collective-permute-start(bf16[3,8,4096]{2,1,0:T(8,128)(2,1)S(1)} %slice.6), channel_id=1, source_target_pairs={{0,2},{2,4},{4,6},{6,8},{8,10},{10,12},{12,14},{14,16},{16,18},{18... | collective-permute-start | bytes 589832 | tf_op jit(solution)/shard_map/ppermute | solution.py:19
  13.0 4.1 %collective-permute-done = bf16[3,8,4096]{2,1,0:T(8,128)(2,1)S(1)} collective-permute-done((bf16[3,8,4096]{2,1,0:T(8,128)(2,1)S(1)}, bf16[3,8,4096]{2,1,0:T(8,128)(2,1)S(1)}, u32[]{:S(2)}, u32[]{:S(2)}) %collective-permute-start) | collective-permute-done | bytes 196640 | tf_op jit(solution)/shard_map/ppermute | solution.py:19
  17.1 1.0 copy-done.2
  18.1 0.9 copy-done.4
  19.1 25.0 %shard_map.104 = (bf16[256,4096]{1,0:T(8,128)(2,1)S(1)}, bf16[256,4096]{1,0:T(8,128)(2,1)S(1)}, bf16[256,4096]{1,0:T(8,128)(2,1)}, bf16[256,4096]{1,0:T(8,128)(2,1)}, bf16[2,16,4096]{2,1,0:T(8,128)(2,1)S(1)}) custom-call(bf16[3,256,4096]{2,1,0:T(8,128)(2,1)} %in_ref.3, f32[3,8,4096]{2,1,0:T(8,128)S(1)} %convert_element_type.6.rim_ref, ...), custom_call_target="tpu_custom_call" | custom-call | flops 115343360 | bytes 18038784 | tf_op jit(solution)/shard_map/pallas_call | solution.py:288
  44.1 1.3 copy-done.7
  45.4 1.4 copy-done.9
  47.5 7.9 %all-to-all-start = ((bf16[16,2,16,256]{3,2,1,0:T(8,128)(2,1)}), bf16[16,2,16,256]{3,2,1,0:T(8,128)(2,1)S(1)}, u32[]{:S(2)}, u32[]{:S(2)}) async-start(bf16[16,2,16,256]{3,2,1,0:T(8,128)(2,1)} %bitcast.9), calls=%async_computation | async-start | bytes 524288 | tf_op jit(solution)/shard_map/all_to_all | solution.py:327
  56.4 12.4 %shard_map.106.spec_ref = f32[512,4096]{1,0:T(8,128)} custom-call(f32[16,4096]{1,0:T(8,128)S(1)} %copy-done.6, f32[16,4096]{1,0:T(8,128)S(1)} %copy-done.5, bf16[512,256]{1,0:T(8,128)(2,1)S(1)} %copy-done.11, bf16[512,256]{1,0:T(8,128)(2,1)S(1)} %copy-done.12), custom_call_target="tpu_custom_call" | custom-call | flops 3221225472 | bytes 9437184 | tf_op jit(solution)/shard_map/pallas_call | solution.py:288
  69.7 7.0 %all-to-all-start.1 = ((bf16[16,2,16,256]{3,2,1,0:T(8,128)(2,1)}), bf16[16,2,16,256]{3,2,1,0:T(8,128)(2,1)}, u32[]{:S(2)}, u32[]{:S(2)}) async-start(bf16[16,2,16,256]{3,2,1,0:T(8,128)(2,1)} %shard_map.105), calls=%async_computation.1 | async-start | bytes 524288 | tf_op jit(solution)/shard_map/all_to_all | solution.py:339
  76.7 1.6 copy-done.8
  78.3 1.6 copy-done.10
  79.9 0.9 copy-done.13
  80.9 0.9 copy-done.14
  82.8 16.3 %shard_map.107 = (f32[256,4096]{1,0:T(8,128)}, f32[256,4096]{1,0:T(8,128)}) custom-call(bf16[256,4096]{1,0:T(8,128)(2,1)S(1)} %copy-done.8, bf16[256,4096]{1,0:T(8,128)(2,1)S(1)} %copy-done.10, f32[512,4096]{1,0:T(8,128)} %shard_map.106.spec_ref, bf16[512,256]{1,0:T(8,128)(2,1)S(1)} %copy-done.11, bf16[512,256]{1,0:T(8,128)(2,1)S(1)} %copy-done.13, ...), custom_call_target="tpu_custom_call" | custom-call | flops 8589934592 | bytes 22020096 | tf_op jit(solution)/shard_map/pallas_call | solution.py:288
  99.0 1.0 copy.15
  100.0 1.6 copy-done.1
  101.6 25.4 %shard_map.108 = (bf16[3,256,4096]{2,1,0:T(8,128)(2,1)}, f32[3,7,4096]{2,1,0:T(8,128)}) custom-call(bf16[2,16,4096]{2,1,0:T(8,128)(2,1)S(1)} %bitcast.10, f32[16,4096]{1,0:T(8,128)S(1)} %copy-done.6, f32[16,4096]{1,0:T(8,128)S(1)} %copy-done.5, f32[256,4096]{1,0:T(8,128)} %get-tuple-element.14.fwd_ref, f32[256,4096]{1,0:T(8,128)} %get-tuple-element.15.back_ref, ...), custom_call_target="tpu_custom_call" | custom-call | flops 115343360 | bytes 28786688 | tf_op jit(solution)/shard_map/pallas_call | solution.py:288
  128.0 1.3 collective-permute-start.1
  129.3 6.3 %collective-permute-done.1 = bf16[3,8,4096]{2,1,0:T(8,128)(2,1)S(1)} collective-permute-done((bf16[3,8,4096]{2,1,0:T(8,128)(2,1)S(1)}, bf16[3,8,4096]{2,1,0:T(8,128)(2,1)S(1)}, u32[]{:S(2)}, u32[]{:S(2)}) %collective-permute-start.1) | collective-permute-done | bytes 196640 | tf_op jit(solution)/shard_map/ppermute | solution.py:19
  135.6 100.7 %all-reduce.2.cloned.1.call-done = f32[3,7,4096]{2,1,0:T(8,128)} async-done(((f32[3,7,4096]{2,1,0:T(8,128)}), f32[3,7,4096]{2,1,0:T(8,128)}) %all-reduce.2.cloned.1.call-update) | async-done | bytes 344080 | tf_op jit(solution)/shard_map/psum | solution.py:349
  236.3 1.7 multiply_reduce_fusion
  238.0 11.1 %shard_map.109 = bf16[3,256,4096]{2,1,0:T(8,128)(2,1)} custom-call(bf16[3,256,4096]{2,1,0:T(8,128)(2,1)} %get-tuple-element.18.gm_ref, f32[3,8,4096]{2,1,0:T(8,128)S(1)} %convert_element_type.7.rim_ref, f32[3,7,4096]{2,1,0:T(8,128)S(1)} %copy-done.3), custom_call_target="tpu_custom_call" | custom-call | flops 44040192 | bytes 13320192 | tf_op jit(solution)/shard_map/pallas_call | solution.py:288
  249.1 3.1 %psum.15 = f32[]{:T(128)} all-reduce(f32[]{:T(128)} %multiply_reduce_fusion), channel_id=1, replica_groups=mesh['ctx'=16,'tp'=2] {'tp'}, use_global_device_ids=true, to_apply=%region_2.0 | all-reduce | flops 1 | bytes 8 | tf_op jit(solution)/shard_map/psum | solution.py:354
  (37 shorter events, 6.3 us)
Async XLA Ops:
  8.1 9.0 %collective-permute-start = (bf16[3,8,4096]{2,1,0:T(8,128)(2,1)S(1)}, bf16[3,8,4096]{2,1,0:T(8,128)(2,1)S(1)}, u32[]{:S(2)}, u32[]{:S(2)}) collective-permute-start(bf16[3,8,4096]{2,1,0:T(8,128)(2,1)S(1)} %slice.6), channel_id=1, source_target_pairs={{0,2},{2,4},{4,6},{6,8},{8,10},{10,12},{12,14},{14,16},{16,18},{18... | collective-permute-start | bytes 589832 | tf_op jit(solution)/shard_map/ppermute | solution.py:19
  17.1 1.0 copy-start.2
  18.1 0.9 copy-start.4
  19.1 36.3 %copy-start.5 = (f32[16,4096]{1,0:T(8,128)S(1)}, f32[16,4096]{1,0:T(8,128)}, u32[]{:S(2)}) copy-start(f32[16,4096]{1,0:T(8,128)} %rate_ref.5) | copy-start | bytes 786436
  19.1 36.3 %copy-start.6 = (f32[16,4096]{1,0:T(8,128)S(1)}, f32[16,4096]{1,0:T(8,128)}, u32[]{:S(2)}) copy-start(f32[16,4096]{1,0:T(8,128)} %res_ref.3) | copy-start | bytes 786436
  19.1 36.3 %copy-start.11 = (bf16[512,256]{1,0:T(8,128)(2,1)S(1)}, bf16[512,256]{1,0:T(8,128)(2,1)}, u32[]{:S(2)}) copy-start(bf16[512,256]{1,0:T(8,128)(2,1)} %constant.30.clone.high_ref) | copy-start | bytes 786436
  44.1 1.3 copy-start.7
  45.4 1.4 copy-start.9
  47.5 21.3 %all-to-all-start = ((bf16[16,2,16,256]{3,2,1,0:T(8,128)(2,1)}), bf16[16,2,16,256]{3,2,1,0:T(8,128)(2,1)S(1)}, u32[]{:S(2)}, u32[]{:S(2)}) async-start(bf16[16,2,16,256]{3,2,1,0:T(8,128)(2,1)} %bitcast.9), calls=%async_computation | async-start | bytes 524288 | tf_op jit(solution)/shard_map/all_to_all | solution.py:327
  55.4 1.0 copy-start.12
  69.7 29.3 %all-to-all-start.1 = ((bf16[16,2,16,256]{3,2,1,0:T(8,128)(2,1)}), bf16[16,2,16,256]{3,2,1,0:T(8,128)(2,1)}, u32[]{:S(2)}, u32[]{:S(2)}) async-start(bf16[16,2,16,256]{3,2,1,0:T(8,128)(2,1)} %shard_map.105), calls=%async_computation.1 | async-start | bytes 524288 | tf_op jit(solution)/shard_map/all_to_all | solution.py:339
  76.7 159.6 %all-reduce.2.cloned.1.call-start = ((), (), s32[]{:S(2)}) async-start(), calls=%async_computation.2 | async-start | bytes 786432 | tf_op jit(solution)/shard_map/psum | solution.py:349
  76.7 1.6 copy-start.8
  78.3 1.6 copy-start.10
  79.9 0.9 copy-start.13
  80.9 0.9 copy-start.14
  81.8 0.9 copy-start.15
  82.8 17.3 %copy-start = (bf16[256,4096]{1,0:T(8,128)(2,1)S(1)}, bf16[256,4096]{1,0:T(8,128)(2,1)}, u32[]{:S(2)}) copy-start(bf16[256,4096]{1,0:T(8,128)(2,1)} %get-tuple-element.16.key_ref) | copy-start | bytes 6291460
  100.0 1.6 copy-start.1
  101.6 136.4 %copy-start.3 = (f32[3,7,4096]{2,1,0:T(8,128)S(1)}, f32[3,7,4096]{2,1,0:T(8,128)}, u32[]{:S(2)}) copy-start(f32[3,7,4096]{2,1,0:T(8,128)} %short_ref.3) | copy-start | bytes 1032196
  128.0 7.6 %collective-permute-start.1 = (bf16[3,8,4096]{2,1,0:T(8,128)(2,1)S(1)}, bf16[3,8,4096]{2,1,0:T(8,128)(2,1)S(1)}, u32[]{:S(2)}, u32[]{:S(2)}) collective-permute-start(bf16[3,8,4096]{2,1,0:T(8,128)(2,1)S(1)} %slice.7), channel_id=1, source_target_pairs={{2,0},{4,2},{6,4},{8,6},{10,8},{12,10},{14,12},{16,14},{18,16},{20... | collective-permute-start | bytes 589832 | tf_op jit(solution)/shard_map/ppermute | solution.py:19
  238.0 14.9 %copy-start.16 = (f32[3,7,4096]{2,1,0:T(8,128)S(1)}, f32[3,7,4096]{2,1,0:T(8,128)}, u32[]{:S(2)}) copy-start(f32[3,7,4096]{2,1,0:T(8,128)} %all-reduce.2.cloned.1.call-done) | copy-start | bytes 1032196
Sparse Core Ops, SparseCore 0:
  127.2 109.0 all-reduce.1
where the time goes:
time: 262 us; the launch traced here: 261 us
  waiting for transfers between devices  111 us (42%)
  Pallas kernels  91.1 us (35%)
  starting transfers between devices  21 us (8%)
  local copies, waits for them, and re-layouts  16.8 us (6%)
  between operations  14.9 us (6%)
  blocking collectives  3.08 us (1%)
    psum x1, waiting for transfers between devices, per_device(): short_sum = lax.psum(short_grad, 'ctx')  101 us
    pallas_call x5, Pallas kernels, over_channels(): pl.pallas_call(kernel, grid=(channels // tile,), in_specs=[tiled(a.shape,...  90.2 us
    unnamed x34, local copies, waits for them, and re-layouts  13.2 us
    ppermute x2, waiting for transfers between devices, passed_along(): return lax.ppermute(shard, axis, pairs)  10.4 us
    all_to_all x1, starting transfers between devices, per_device(): lax.all_to_all(sent, 'ctx', split_axis=0, concat_axis=0, tiled=True)  7.86 us
    all_to_all x1, starting transfers between devices, per_device(): lax.all_to_all(bounds, 'ctx', split_axis=0, concat_axis=0, tiled=True)  6.95 us
    ppermute x2, starting transfers between devices, passed_along(): return lax.ppermute(shard, axis, pairs)  6.15 us
  transfers between devices with their start and end apart: 5, of which 3 were waited for; matrix products, arithmetic and copies ran while one was open for 0% of the time, Pallas kernels for 11%

commit v1 on v0

--- a/solution.py
+++ b/solution.py
@@ -10,7 +10,7 @@
 
 LANES = 128
 RIM = 8
-VMEM_LIMIT = 48 * 1024 * 1024
+VMEM_LIMIT = 60 * 1024 * 1024
 
 
 def passed_along(shard, axis, by):
@@ -318,6 +318,7 @@
         [shape((2 * rows, channels), f32)], [pltpu.VMEM((rows, tile), f32)], tile,
         6 * 2 * rows * rows * channels,
     )
+    rim, spec = lax.optimization_barrier((rim, spec))
     gated, grad_mixer, key_mix, value_mix, states = over_channels(
         mix_kernel, [inputs, rim, cotangent, short_filter, decay_rate], [],
         [shape((rows, channels), bf16)] * 4 + [shape((2, modes, channels), bf16)],
@@ -345,13 +346,22 @@
         [shape((3, rows, channels), bf16), shape((3, taps, channels), f32)],
         [ext_rows, pltpu.VMEM((2, rows, LANES), f32)], tile, 110 * rows * channels,
     )
-    next_rim = passed_along(grad_mix[:, :RIM, :], "ctx", -1).astype(f32)
-    short_sum = lax.psum(short_grad, "ctx")
+    next_rim = passed_along(grad_mix[:, :RIM, :], "ctx", -1)
+    terms = short_grad.reshape(3 * taps, ctx_count, narrow).transpose(1, 0, 2)
+    terms = lax.all_to_all(terms, "ctx", split_axis=0, concat_axis=0, tiled=True)
+    next_rim, terms = lax.optimization_barrier((next_rim, terms))
+    next_rim = next_rim.astype(f32)
+    own_sum = jnp.sum(terms, axis=0)
+    own_squares = jnp.broadcast_to(jnp.sum(own_sum * own_sum), (1, narrow))
+    packed = jnp.concatenate([own_sum, own_squares], axis=0)
+    packed = jnp.broadcast_to(packed[None], (ctx_count,) + packed.shape)
+    packed = lax.all_to_all(packed, "ctx", split_axis=0, concat_axis=0, tiled=True)
+    short_sum = packed[:, : 3 * taps].transpose(1, 0, 2).reshape(3, taps, channels)
     (grad_inputs,) = over_channels(
         spread_kernel, [grad_mix, next_rim, short_filter], [],
         [shape((3, rows, channels), bf16)], [ext_rows], tile, 42 * rows * channels,
     )
-    squares = lax.psum(jnp.sum(short_sum * short_sum), "tp")
+    squares = lax.psum(jnp.sum(packed[:, 3 * taps, 0]), "tp")
     clip_limit = math.sqrt(3 * channels * lax.axis_size("tp") * taps)
     factor = jnp.minimum(1.0, clip_limit / (jnp.sqrt(squares) + 1e-06))
     return (grad_inputs, short_sum * factor)

time: 262 us -> 170 us (0.65)
  waiting for transfers between devices: 111 us -> 27.9 us
  between operations: 14.9 us -> 1.46 us
  starting transfers between devices: 21 us -> 29.4 us
  local copies, waits for them, and re-layouts: 16.8 us -> 9.53 us
    psum x1 -> x0, waiting for transfers between devices: 101 us -> none  [per_device(): short_sum = lax.psum(short_grad, 'ctx')]
    all_to_all x0 -> x2, starting transfers between devices: none -> 13.8 us  [the longest x1 6.89 us: per_device(): lax.all_to_all(packed, 'ctx', split_axis=0, concat_axis=0, tiled=True)]
    unnamed x34 -> x2, local copies, waits for them, and re-layouts: 13.2 us -> 0.7 us
    all_to_all x0 -> x2, waiting for transfers between devices: none -> 10.9 us  [the longest x1 10.5 us: per_device(): lax.all_to_all(packed, 'ctx', split_axis=0, concat_axis=0, tiled=True)]
    all_to_all x1, waiting for transfers between devices: 0.01 us -> 8.26 us  [per_device(): lax.all_to_all(sent, 'ctx', split_axis=0, concat_axis=0, tiled=True)]
    all_to_all x1, starting transfers between devices: 6.95 us -> 3.55 us  [per_device(): lax.all_to_all(bounds, 'ctx', split_axis=0, concat_axis=0, tiled=True)]
  transfers between devices with their start and end apart: 5 -> 6, of which waited for: 3 -> 4; matrix products, arithmetic and copies ran while one was open for 0% -> 2% of each run, Pallas kernels for 11% -> 18%
where the time goes in v1:
time: 170 us; the launch traced here: 169 us
  Pallas kernels  93.1 us (55%)
  starting transfers between devices  29.4 us (17%)
  waiting for transfers between devices  27.9 us (16%)
  local copies, waits for them, and re-layouts  9.53 us (6%)
  other arithmetic  4.18 us (2%)
  blocking collectives  3.08 us (2%)
    pallas_call x5, Pallas kernels, over_channels(): pl.pallas_call(kernel, grid=(channels // tile,), in_specs=[tiled(a.shape,...  91.3 us
    all_to_all x1, waiting for transfers between devices, per_device(): lax.all_to_all(packed, 'ctx', split_axis=0, concat_axis=0, tiled=True)  10.5 us
    ppermute x2, waiting for transfers between devices, passed_along(): return lax.ppermute(shard, axis, pairs)  8.8 us
    all_to_all x1, waiting for transfers between devices, per_device(): lax.all_to_all(sent, 'ctx', split_axis=0, concat_axis=0, tiled=True)  8.26 us
    all_to_all x1, starting transfers between devices, per_device(): lax.all_to_all(packed, 'ctx', split_axis=0, concat_axis=0, tiled=True)  6.89 us
    all_to_all x1, starting transfers between devices, per_device(): lax.all_to_all(terms, 'ctx', split_axis=0, concat_axis=0, tiled=True)  6.89 us
    ppermute x2, starting transfers between devices, passed_along(): return lax.ppermute(shard, axis, pairs)  6.15 us
    all_to_all x1, starting transfers between devices, per_device(): lax.all_to_all(sent, 'ctx', split_axis=0, concat_axis=0, tiled=True)  5.93 us
  transfers between devices with their start and end apart: 6, of which 4 were waited for; matrix products, arithmetic and copies ran while one was open for 2% of the time, Pallas kernels for 18%

profile of v1, /device:TPU:0, one launch (start us, length us, event | category | flops | bytes accessed | tf_op | source)
XLA Modules:
  0.0 168.7 jit_solution(14723665056086745326)
XLA Ops:
  0.6 0.9 slice.12
  1.6 4.9 %collective-permute-start = (bf16[3,8,4096]{2,1,0:T(8,128)(2,1)S(1)}, bf16[3,8,4096]{2,1,0:T(8,128)(2,1)S(1)}, u32[]{:S(2)}, u32[]{:S(2)}) collective-permute-start(bf16[3,8,4096]{2,1,0:T(8,128)(2,1)S(1)} %slice.12), channel_id=1, source_target_pairs={{0,2},{2,4},{4,6},{6,8},{8,10},{10,12},{12,14},{14,16},{16,18},{18... | collective-permute-start | bytes 589832 | tf_op jit(solution)/shard_map/ppermute | solution.py:19
  6.4 13.6 %shard_map.104.spec_ref = f32[512,4096]{1,0:T(8,128)} custom-call(f32[16,4096]{1,0:T(8,128)} %res_ref.3, f32[16,4096]{1,0:T(8,128)} %rate_ref.5, bf16[512,256]{1,0:T(8,128)(2,1)} %constant.30.clone.high_ref, bf16[512,256]{1,0:T(8,128)(2,1)} %constant.31.clone.low_ref), custom_call_target="tpu_custom_call" | custom-call | flops 3221225472 | bytes 9437184 | tf_op jit(solution)/shard_map/pallas_call | solution.py:288
  20.0 0.8 convert_element_type.6.rim_ref
  20.8 24.7 %shard_map.105 = (bf16[256,4096]{1,0:T(8,128)(2,1)}, bf16[256,4096]{1,0:T(8,128)(2,1)}, bf16[256,4096]{1,0:T(8,128)(2,1)}, bf16[256,4096]{1,0:T(8,128)(2,1)}, bf16[2,16,4096]{2,1,0:T(8,128)(2,1)}) custom-call(bf16[3,256,4096]{2,1,0:T(8,128)(2,1)} %in_ref.3, f32[3,8,4096]{2,1,0:T(8,128)} %convert_element_type.6.rim_ref, bf16[256,4096]{1,0:T(8,128)(2,1)} %cot_ref.3, ...), custom_call_target="tpu_custom_call" | custom-call | flops 115343360 | bytes 18038784 | tf_op jit(solution)/shard_map/pallas_call | solution.py:288
  45.5 1.7 %copy.26 = bf16[2,2,16,8,256]{4,3,1,0,2:T(8,128)(2,1)} copy(bf16[2,2,16,8,256]{4,3,2,1,0:T(8,128)(2,1)} %bitcast.17) | data formatting | bytes 524288 | tf_op jit(solution)/shard_map/reshape | solution.py:327
  47.2 5.9 %all-to-all-start = ((bf16[16,2,16,256]{3,2,1,0:T(8,128)(2,1)}), bf16[16,2,16,256]{3,2,1,0:T(8,128)(2,1)S(1)}, u32[]{:S(2)}, u32[]{:S(2)}) async-start(bf16[16,2,16,256]{3,2,1,0:T(8,128)(2,1)} %bitcast.14), calls=%async_computation | async-start | bytes 524288 | tf_op jit(solution)/shard_map/all_to_all | solution.py:328
  53.2 1.3 multiply_exponential_fusion.step_ref
  54.5 8.3 %all-to-all-done.states_ref = bf16[16,2,16,256]{3,2,1,0:T(8,128)(2,1)S(1)} async-done(((bf16[16,2,16,256]{3,2,1,0:T(8,128)(2,1)}), bf16[16,2,16,256]{3,2,1,0:T(8,128)(2,1)S(1)}, u32[]{:S(2)}, u32[]{:S(2)}) %all-to-all-start) | async-done | bytes 262176 | tf_op jit(solution)/shard_map/all_to_all | solution.py:328
  63.4 1.8 %shard_map.106 = bf16[16,2,16,256]{3,2,1,0:T(8,128)(2,1)} custom-call(bf16[16,2,16,256]{3,2,1,0:T(8,128)(2,1)} %copy-done, f32[16,256]{1,0:T(8,128)} %multiply_exponential_fusion.step_ref), custom_call_target="tpu_custom_call" | custom-call | tf_op jit(solution)/shard_map/pallas_call | solution.py:335
  65.3 3.5 %all-to-all-start.1 = ((bf16[16,2,16,256]{3,2,1,0:T(8,128)(2,1)}), bf16[16,2,16,256]{3,2,1,0:T(8,128)(2,1)S(1)}, u32[]{:S(2)}, u32[]{:S(2)}) async-start(bf16[16,2,16,256]{3,2,1,0:T(8,128)(2,1)} %shard_map.106), calls=%async_computation.1 | async-start | bytes 524288 | tf_op jit(solution)/shard_map/all_to_all | solution.py:340
  68.8 16.5 %shard_map.107 = (f32[256,4096]{1,0:T(8,128)}, f32[256,4096]{1,0:T(8,128)}) custom-call(bf16[256,4096]{1,0:T(8,128)(2,1)} %get-tuple-element.17.gated_ref, bf16[256,4096]{1,0:T(8,128)(2,1)} %get-tuple-element.18.grad_ref, f32[512,4096]{1,0:T(8,128)} %shard_map.104.spec_ref, bf16[512,256]{1,0:T(8,128)(2,1)} %constant.30.clone.high_ref, ...), custom_call_target="tpu_custom_call" | custom-call | flops 8589934592 | bytes 22020096 | tf_op jit(solution)/shard_map/pallas_call | solution.py:288
  86.1 25.3 %shard_map.108 = (bf16[3,256,4096]{2,1,0:T(8,128)(2,1)}, f32[3,7,4096]{2,1,0:T(8,128)}) custom-call(bf16[2,16,4096]{2,1,0:T(8,128)(2,1)} %bitcast.15, f32[16,4096]{1,0:T(8,128)} %res_ref.3, f32[16,4096]{1,0:T(8,128)} %rate_ref.5, f32[256,4096]{1,0:T(8,128)} %get-tuple-element.20.fwd_ref, f32[256,4096]{1,0:T(8,128)} %get-tuple-element.21.back_ref, ...), custom_call_target="tpu_custom_call" | custom-call | flops 115343360 | bytes 28786688 | tf_op jit(solution)/shard_map/pallas_call | solution.py:288
  111.4 1.2 reshape.19
  112.6 1.0 copy.25
  113.5 6.9 %all-to-all-start.2 = ((f32[16,21,256]{2,1,0:T(8,128)}), f32[16,21,256]{2,1,0:T(8,128)S(1)}, u32[]{:S(2)}, u32[]{:S(2)}) async-start(f32[16,21,256]{2,1,0:T(8,128)} %bitcast.12), calls=%async_computation.2 | async-start | bytes 786432 | tf_op jit(solution)/shard_map/all_to_all | solution.py:351
  120.4 0.9 slice.13
  121.4 1.3 collective-permute-start.1
  122.7 8.8 %collective-permute-done.1 = bf16[3,8,4096]{2,1,0:T(8,128)(2,1)S(1)} collective-permute-done((bf16[3,8,4096]{2,1,0:T(8,128)(2,1)S(1)}, bf16[3,8,4096]{2,1,0:T(8,128)(2,1)S(1)}, u32[]{:S(2)}, u32[]{:S(2)}) %collective-permute-start.1) | collective-permute-done | bytes 196640 | tf_op jit(solution)/shard_map/ppermute | solution.py:19
  134.0 6.9 %all-to-all-start.3 = ((f32[16,22,256]{2,1,0:T(8,128)}), f32[16,22,256]{2,1,0:T(8,128)S(1)}, u32[]{:S(2)}, u32[]{:S(2)}) async-start(f32[16,22,256]{2,1,0:T(8,128)} %broadcast_in_dim.2), calls=%async_computation.3 | async-start | bytes 786432 | tf_op jit(solution)/shard_map/all_to_all | solution.py:358
  141.6 10.5 %all-to-all-done.3 = f32[16,22,256]{2,1,0:T(8,128)S(1)} async-done(((f32[16,22,256]{2,1,0:T(8,128)}), f32[16,22,256]{2,1,0:T(8,128)S(1)}, u32[]{:S(2)}, u32[]{:S(2)}) %all-to-all-start.3) | async-done | bytes 360480 | tf_op jit(solution)/shard_map/all_to_all | solution.py:358
  152.7 11.2 %shard_map.109 = bf16[3,256,4096]{2,1,0:T(8,128)(2,1)} custom-call(bf16[3,256,4096]{2,1,0:T(8,128)(2,1)} %get-tuple-element.24.gm_ref, f32[3,8,4096]{2,1,0:T(8,128)} %convert_element_type.7.rim_ref, f32[3,7,4096]{2,1,0:T(8,128)} %short_ref.3), custom_call_target="tpu_custom_call" | custom-call | flops 44040192 | bytes 13320192 | tf_op jit(solution)/shard_map/pallas_call | solution.py:288
  163.9 3.1 %psum.7 = f32[]{:T(128)} all-reduce(f32[]{:T(128)} %slice_reduce_fusion), channel_id=1, replica_groups=mesh['ctx'=16,'tp'=2] {'tp'}, use_global_device_ids=true, to_apply=%region_3.0 | all-reduce | flops 1 | bytes 8 | tf_op jit(solution)/shard_map/psum | solution.py:364
  167.9 0.9 mul.31
  (14 shorter events, 5.5 us)
Async XLA Ops:
  1.6 18.4 %collective-permute-start = (bf16[3,8,4096]{2,1,0:T(8,128)(2,1)S(1)}, bf16[3,8,4096]{2,1,0:T(8,128)(2,1)S(1)}, u32[]{:S(2)}, u32[]{:S(2)}) collective-permute-start(bf16[3,8,4096]{2,1,0:T(8,128)(2,1)S(1)} %slice.12), channel_id=1, source_target_pairs={{0,2},{2,4},{4,6},{6,8},{8,10},{10,12},{12,14},{14,16},{16,18},{18... | collective-permute-start | bytes 589832 | tf_op jit(solution)/shard_map/ppermute | solution.py:19
  47.2 15.5 %all-to-all-start = ((bf16[16,2,16,256]{3,2,1,0:T(8,128)(2,1)}), bf16[16,2,16,256]{3,2,1,0:T(8,128)(2,1)S(1)}, u32[]{:S(2)}, u32[]{:S(2)}) async-start(bf16[16,2,16,256]{3,2,1,0:T(8,128)(2,1)} %bitcast.14), calls=%async_computation | async-start | bytes 524288 | tf_op jit(solution)/shard_map/all_to_all | solution.py:328
  62.7 0.7 copy-start
  65.3 20.1 %all-to-all-start.1 = ((bf16[16,2,16,256]{3,2,1,0:T(8,128)(2,1)}), bf16[16,2,16,256]{3,2,1,0:T(8,128)(2,1)S(1)}, u32[]{:S(2)}, u32[]{:S(2)}) async-start(bf16[16,2,16,256]{3,2,1,0:T(8,128)(2,1)} %shard_map.106), calls=%async_computation.1 | async-start | bytes 524288 | tf_op jit(solution)/shard_map/all_to_all | solution.py:340
  113.5 18.4 %all-to-all-start.2 = ((f32[16,21,256]{2,1,0:T(8,128)}), f32[16,21,256]{2,1,0:T(8,128)S(1)}, u32[]{:S(2)}, u32[]{:S(2)}) async-start(f32[16,21,256]{2,1,0:T(8,128)} %bitcast.12), calls=%async_computation.2 | async-start | bytes 786432 | tf_op jit(solution)/shard_map/all_to_all | solution.py:351
  121.4 10.1 %collective-permute-start.1 = (bf16[3,8,4096]{2,1,0:T(8,128)(2,1)S(1)}, bf16[3,8,4096]{2,1,0:T(8,128)(2,1)S(1)}, u32[]{:S(2)}, u32[]{:S(2)}) collective-permute-start(bf16[3,8,4096]{2,1,0:T(8,128)(2,1)S(1)} %slice.13), channel_id=1, source_target_pairs={{2,0},{4,2},{6,4},{8,6},{10,8},{12,10},{14,12},{16,14},{18,16},{20... | collective-permute-start | bytes 589832 | tf_op jit(solution)/shard_map/ppermute | solution.py:19
  134.0 18.1 %all-to-all-start.3 = ((f32[16,22,256]{2,1,0:T(8,128)}), f32[16,22,256]{2,1,0:T(8,128)S(1)}, u32[]{:S(2)}, u32[]{:S(2)}) async-start(f32[16,22,256]{2,1,0:T(8,128)} %broadcast_in_dim.2), calls=%async_computation.3 | async-start | bytes 786432 | tf_op jit(solution)/shard_map/all_to_all | solution.py:358

commit v2 on v1

--- a/solution.py
+++ b/solution.py
@@ -1,3 +1,4 @@
+import functools
 import math
 
 import jax
@@ -87,7 +88,7 @@
 
 def mix_kernel(
     in_ref, rim_ref, cot_ref, short_ref, rate_ref,
-    gated_ref, grad_ref, key_ref, value_ref, state_ref, ext, rowed,
+    gated_ref, grad_ref, key_ref, value_ref, state_ref, rowed,
 ):
     rows, width = cot_ref.shape
     modes = rate_ref.shape[0]
@@ -98,14 +99,19 @@
     @pl.loop(0, width // LANES)
     def _(chunk):
         lanes = pl.ds(pl.multiple_of(chunk * LANES, LANES), LANES)
-        fill_extended(ext, in_ref, rim_ref, lanes)
         for first in range(0, rows, part):
             mixed = []
             for i in range(3):
-                total = None
-                for j in range(taps):
-                    term = short_ref[i, j : j + 1, lanes] * ext[i, first + RIM - j : first + RIM - j + part, :]
-                    total = term if total is None else total + term
+                own = in_ref[i, first : first + part, lanes].astype(jnp.float32)
+                if first > 0:
+                    prior = in_ref[i, first - 16 : first, lanes].astype(jnp.float32)[16 - RIM : 16]
+                else:
+                    prior = rim_ref[i, :, lanes]
+                both = jnp.concatenate([prior, own], axis=0)
+                total = short_ref[i, 0:1, lanes] * own
+                for j in range(1, taps):
+                    moved = pltpu.roll(both, j, 0)[RIM : RIM + part]
+                    total = total + short_ref[i, j : j + 1, lanes] * moved
                 mixed.append(total)
             here = slice(first, first + part)
             gated_ref[here, lanes] = (mixed[1] * mixed[2]).astype(jnp.bfloat16)
@@ -142,26 +148,20 @@
         state_ref[1, :, lanes] = rowed[modes : 2 * modes, :].astype(jnp.bfloat16)
 
 
-def local_kernel(gated_ref, grad_ref, spec_ref, high_ref, low_ref, hight_ref, lowt_ref, fwd_ref, back_ref):
-    rows = gated_ref.shape[0]
+def local_kernel(sign, signal_ref, spec_ref, high_ref, low_ref, hight_ref, lowt_ref, out_ref):
+    rows = signal_ref.shape[0]
     real = spec_ref[0:rows, :]
     lower = spec_ref[rows : 2 * rows, :]
     first = lax.broadcasted_iota(jnp.int32, real.shape, 0) == 0
-    imag = jnp.where(first, 0.0, lower)
+    imag = sign * jnp.where(first, 0.0, lower)
     other = jnp.where(first, lower, real)
-
-    def convolved(signal, sign, out_ref):
-        seen = mm(high_ref[...], signal) + mm(low_ref[...], signal)
-        a = seen[0:rows, :]
-        b = seen[rows : 2 * rows, :]
-        imag_s = imag * sign
-        top = (a * real - b * imag_s).astype(jnp.bfloat16)
-        bottom = (a * imag_s + b * other).astype(jnp.bfloat16)
-        both = jnp.concatenate([top, bottom], axis=0)
-        out_ref[...] = mm(hight_ref[...], both) + mm(lowt_ref[...], both)
-
-    convolved(gated_ref[...], 1.0, fwd_ref)
-    convolved(grad_ref[...], -1.0, back_ref)
+    seen = mm(high_ref[...], signal_ref[...]) + mm(low_ref[...], signal_ref[...])
+    a = seen[0:rows, :]
+    b = seen[rows : 2 * rows, :]
+    top = (a * real - b * imag).astype(jnp.bfloat16)
+    bottom = (a * imag + b * other).astype(jnp.bfloat16)
+    both = jnp.concatenate([top, bottom], axis=0)
+    out_ref[...] = mm(hight_ref[...], both) + mm(lowt_ref[...], both)
 
 
 def scan_kernel(states_ref, step_ref, out_ref):
@@ -252,24 +252,28 @@
                 short_ref[i, j : j + 1, lanes] = jnp.sum(sums[i][j], axis=0, keepdims=True)
 
 
-def spread_kernel(gm_ref, rim_ref, short_ref, out_ref, ext):
+def spread_kernel(gm_ref, rim_ref, short_ref, out_ref):
     rows, width = gm_ref.shape[1:]
     taps = short_ref.shape[1]
-    part = 32
+    part = 64
 
     @pl.loop(0, width // LANES)
     def _(chunk):
         lanes = pl.ds(pl.multiple_of(chunk * LANES, LANES), LANES)
-        for i in range(3):
-            ext[i, 0:rows, :] = gm_ref[i, :, lanes].astype(jnp.float32)
-            ext[i, rows : rows + RIM, :] = rim_ref[i, :, lanes]
         for first in range(0, rows, part):
+            end = first + part
             for i in range(3):
-                total = None
-                for j in range(taps):
-                    term = short_ref[i, j : j + 1, lanes] * ext[i, first + j : first + j + part, :]
-                    total = term if total is None else total + term
-                out_ref[i, first : first + part, lanes] = total.astype(jnp.bfloat16)
+                own = gm_ref[i, first:end, lanes].astype(jnp.float32)
+                if end < rows:
+                    beyond = gm_ref[i, end : end + 16, lanes].astype(jnp.float32)[0:RIM]
+                else:
+                    beyond = rim_ref[i, :, lanes]
+                both = jnp.concatenate([own, beyond], axis=0)
+                total = short_ref[i, 0:1, lanes] * own
+                for j in range(1, taps):
+                    moved = pltpu.roll(both, part + RIM - j, 0)[0:part]
+                    total = total + short_ref[i, j : j + 1, lanes] * moved
+                out_ref[i, first:end, lanes] = total.astype(jnp.bfloat16)
 
 
 def tiled(shape, tile):
@@ -322,14 +326,18 @@
     gated, grad_mixer, key_mix, value_mix, states = over_channels(
         mix_kernel, [inputs, rim, cotangent, short_filter, decay_rate], [],
         [shape((rows, channels), bf16)] * 4 + [shape((2, modes, channels), bf16)],
-        [ext_rows, pltpu.VMEM((2 * modes, LANES), f32)], tile, 110 * rows * channels,
+        [pltpu.VMEM((2 * modes, LANES), f32)], tile, 110 * rows * channels,
     )
     sent = states.reshape(2, modes, ctx_count, narrow).transpose(2, 0, 1, 3)
     arrived = lax.all_to_all(sent, "ctx", split_axis=0, concat_axis=0, tiled=True)
-    fwd_part, back_part = over_channels(
-        local_kernel, [gated, grad_mixer, spec], tables + turned,
-        [shape((rows, channels), f32)] * 2, [], tile, 16 * 2 * rows * rows * channels,
-    )
+    def local(sign, signal):
+        return over_channels(
+            functools.partial(local_kernel, sign), [signal, spec], tables + turned,
+            [shape((rows, channels), f32)], [], tile, 8 * 2 * rows * rows * channels,
+        )[0]
+
+    fwd_part = local(1.0, gated)
+    arrived, fwd_part = lax.optimization_barrier((arrived, fwd_part))
     first_chan = lax.axis_index("ctx") * narrow
     rate_part = lax.dynamic_slice_in_dim(decay_rate, first_chan, narrow, 1)
     bounds = pl.pallas_call(
@@ -338,6 +346,8 @@
         compiler_params=pltpu.CompilerParams(vmem_limit_bytes=VMEM_LIMIT),
     )(arrived, jnp.exp(-rate_part * rows))
     returned = lax.all_to_all(bounds, "ctx", split_axis=0, concat_axis=0, tiled=True)
+    back_part = local(-1.0, grad_mixer)
+    returned, back_part = lax.optimization_barrier((returned, back_part))
     bound = returned.transpose(1, 2, 0, 3).reshape(2, modes, channels)
     grad_mix, short_grad = over_channels(
         apply_kernel,
@@ -356,11 +366,12 @@
     packed = jnp.concatenate([own_sum, own_squares], axis=0)
     packed = jnp.broadcast_to(packed[None], (ctx_count,) + packed.shape)
     packed = lax.all_to_all(packed, "ctx", split_axis=0, concat_axis=0, tiled=True)
-    short_sum = packed[:, : 3 * taps].transpose(1, 0, 2).reshape(3, taps, channels)
     (grad_inputs,) = over_channels(
         spread_kernel, [grad_mix, next_rim, short_filter], [],
-        [shape((3, rows, channels), bf16)], [ext_rows], tile, 42 * rows * channels,
-    )
+        [shape((3, rows, channels), bf16)], [], tile, 42 * rows * channels,
+    )
+    packed, grad_inputs = lax.optimization_barrier((packed, grad_inputs))
+    short_sum = packed[:, : 3 * taps].transpose(1, 0, 2).reshape(3, taps, channels)
     squares = lax.psum(jnp.sum(packed[:, 3 * taps, 0]), "tp")
     clip_limit = math.sqrt(3 * channels * lax.axis_size("tp") * taps)
     factor = jnp.minimum(1.0, clip_limit / (jnp.sqrt(squares) + 1e-06))

time: 170 us -> 169 us (level)
  waiting for transfers between devices: 27.9 us -> 8.99 us
  Pallas kernels: 93.1 us -> 108 us
  starting transfers between devices: 29.4 us -> 32.8 us
    pallas_call x5 -> x6, Pallas kernels: 91.3 us -> 106 us  [over_channels(): pl.pallas_call(kernel, grid=(channels // tile,), in_specs=[tiled(a.shape,...]
    all_to_all x1, waiting for transfers between devices: 10.5 us -> 0.01 us  [per_device(): lax.all_to_all(packed, 'ctx', split_axis=0, concat_axis=0, tiled=True)]
    all_to_all x1, waiting for transfers between devices: 8.26 us -> 0.01 us  [per_device(): lax.all_to_all(sent, 'ctx', split_axis=0, concat_axis=0, tiled=True)]
    all_to_all x1, starting transfers between devices: 3.55 us -> 6.9 us  [per_device(): lax.all_to_all(bounds, 'ctx', split_axis=0, concat_axis=0, tiled=True)]
  transfers between devices with their start and end apart: 6 -> 6, of which waited for: 4 -> 2; matrix products, arithmetic and copies ran while one was open for 2% -> 2% of each run, Pallas kernels for 18% -> 31%
where the time goes in v2:
time: 169 us; the launch traced here: 168 us
  Pallas kernels  108 us (64%)
  starting transfers between devices  32.8 us (19%)
  local copies, waits for them, and re-layouts  9.57 us (6%)
  waiting for transfers between devices  8.99 us (5%)
  other arithmetic  4.17 us (2%)
  blocking collectives  3.08 us (2%)
    pallas_call x6, Pallas kernels, over_channels(): pl.pallas_call(kernel, grid=(channels // tile,), in_specs=[tiled(a.shape,...  106 us
    ppermute x2, waiting for transfers between devices, passed_along(): return lax.ppermute(shard, axis, pairs)  8.73 us
    all_to_all x1, starting transfers between devices, per_device(): lax.all_to_all(packed, 'ctx', split_axis=0, concat_axis=0, tiled=True)  6.97 us
    all_to_all x1, starting transfers between devices, per_device(): lax.all_to_all(bounds, 'ctx', split_axis=0, concat_axis=0, tiled=True)  6.9 us
    all_to_all x1, starting transfers between devices, per_device(): lax.all_to_all(terms, 'ctx', split_axis=0, concat_axis=0, tiled=True)  6.89 us
    ppermute x2, starting transfers between devices, passed_along(): return lax.ppermute(shard, axis, pairs)  6.15 us
    all_to_all x1, starting transfers between devices, per_device(): lax.all_to_all(sent, 'ctx', split_axis=0, concat_axis=0, tiled=True)  5.93 us
  transfers between devices with their start and end apart: 6, of which 2 were waited for; matrix products, arithmetic and copies ran while one was open for 2% of the time, Pallas kernels for 31%

profile of v2, /device:TPU:0, one launch (start us, length us, event | category | flops | bytes accessed | tf_op | source)
XLA Modules:
  0.0 168.1 jit_solution(14894059094603876733)
XLA Ops:
  0.6 0.9 slice.12
  1.6 4.9 %collective-permute-start = (bf16[3,8,4096]{2,1,0:T(8,128)(2,1)S(1)}, bf16[3,8,4096]{2,1,0:T(8,128)(2,1)S(1)}, u32[]{:S(2)}, u32[]{:S(2)}) collective-permute-start(bf16[3,8,4096]{2,1,0:T(8,128)(2,1)S(1)} %slice.12), channel_id=1, source_target_pairs={{0,2},{2,4},{4,6},{6,8},{8,10},{10,12},{12,14},{14,16},{16,18},{18... | collective-permute-start | bytes 589832 | tf_op jit(solution)/shard_map/ppermute | solution.py:20
  6.4 13.7 %shard_map.104.spec_ref = f32[512,4096]{1,0:T(8,128)} custom-call(f32[16,4096]{1,0:T(8,128)} %res_ref.3, f32[16,4096]{1,0:T(8,128)} %rate_ref.5, bf16[512,256]{1,0:T(8,128)(2,1)} %constant.30.clone.high_ref, bf16[512,256]{1,0:T(8,128)(2,1)} %constant.31.clone.low_ref), custom_call_target="tpu_custom_call" | custom-call | flops 3221225472 | bytes 9437184 | tf_op jit(solution)/shard_map/pallas_call | solution.py:292
  20.1 0.8 convert_element_type.6.rim_ref
  20.9 29.4 %shard_map.105 = (bf16[256,4096]{1,0:T(8,128)(2,1)}, bf16[256,4096]{1,0:T(8,128)(2,1)}, bf16[256,4096]{1,0:T(8,128)(2,1)}, bf16[256,4096]{1,0:T(8,128)(2,1)}, bf16[2,16,4096]{2,1,0:T(8,128)(2,1)}) custom-call(bf16[3,256,4096]{2,1,0:T(8,128)(2,1)} %in_ref.3, f32[3,8,4096]{2,1,0:T(8,128)} %convert_element_type.6.rim_ref, bf16[256,4096]{1,0:T(8,128)(2,1)} %cot_ref.3, ...), custom_call_target="tpu_custom_call" | custom-call | flops 115343360 | bytes 18038784 | tf_op jit(solution)/shard_map/pallas_call | solution.py:292
  50.3 1.7 %copy.26 = bf16[2,2,16,8,256]{4,3,1,0,2:T(8,128)(2,1)} copy(bf16[2,2,16,8,256]{4,3,2,1,0:T(8,128)(2,1)} %bitcast.17) | data formatting | bytes 524288 | tf_op jit(solution)/shard_map/reshape | solution.py:331
  52.0 5.9 %all-to-all-start = ((bf16[16,2,16,256]{3,2,1,0:T(8,128)(2,1)}), bf16[16,2,16,256]{3,2,1,0:T(8,128)(2,1)S(1)}, u32[]{:S(2)}, u32[]{:S(2)}) async-start(bf16[16,2,16,256]{3,2,1,0:T(8,128)(2,1)} %bitcast.14), calls=%async_computation | async-start | bytes 524288 | tf_op jit(solution)/shard_map/all_to_all | solution.py:332
  57.9 1.3 multiply_exponential_fusion.step_ref
  59.2 11.8 %shard_map.106.fwd_ref = f32[256,4096]{1,0:T(8,128)} custom-call(bf16[256,4096]{1,0:T(8,128)(2,1)} %get-tuple-element.21.signal_ref, f32[512,4096]{1,0:T(8,128)} %shard_map.104.spec_ref, bf16[512,256]{1,0:T(8,128)(2,1)} %constant.30.clone.high_ref, bf16[512,256]{1,0:T(8,128)(2,1)} %constant.31.clone.low_ref, bf16[256,512]{1,0:T(8,128)(2,1)} %constant.32.clone.hight_ref, ...), custom_call_target="tpu_custom_call" | custom-call | flops 4294967296 | bytes 15728640 | tf_op jit(solution)/shard_map/pallas_call | solution.py:292
  71.8 1.8 %shard_map.107 = bf16[16,2,16,256]{3,2,1,0:T(8,128)(2,1)} custom-call(bf16[16,2,16,256]{3,2,1,0:T(8,128)(2,1)} %copy-done, f32[16,256]{1,0:T(8,128)} %multiply_exponential_fusion.step_ref), custom_call_target="tpu_custom_call" | custom-call | tf_op jit(solution)/shard_map/pallas_call | solution.py:343
  73.6 6.9 %all-to-all-start.1 = ((bf16[16,2,16,256]{3,2,1,0:T(8,128)(2,1)}), bf16[16,2,16,256]{3,2,1,0:T(8,128)(2,1)S(1)}, u32[]{:S(2)}, u32[]{:S(2)}) async-start(bf16[16,2,16,256]{3,2,1,0:T(8,128)(2,1)} %shard_map.107), calls=%async_computation.1 | async-start | bytes 524288 | tf_op jit(solution)/shard_map/all_to_all | solution.py:348
  80.5 12.1 %shard_map.108.back_ref = f32[256,4096]{1,0:T(8,128)} custom-call(bf16[256,4096]{1,0:T(8,128)(2,1)} %get-tuple-element.24.signal_ref, f32[512,4096]{1,0:T(8,128)} %shard_map.104.spec_ref, bf16[512,256]{1,0:T(8,128)(2,1)} %constant.30.clone.high_ref, bf16[512,256]{1,0:T(8,128)(2,1)} %constant.31.clone.low_ref, bf16[256,512]{1,0:T(8,128)(2,1)} %constant.32.clone.hight_ref, ...), custom_call_target="tpu_custom_call" | custom-call | flops 4294967296 | bytes 15728640 | tf_op jit(solution)/shard_map/pallas_call | solution.py:292
  93.4 25.4 %shard_map.109 = (bf16[3,256,4096]{2,1,0:T(8,128)(2,1)}, f32[3,7,4096]{2,1,0:T(8,128)}) custom-call(bf16[2,16,4096]{2,1,0:T(8,128)(2,1)} %bitcast.15, f32[16,4096]{1,0:T(8,128)} %res_ref.3, f32[16,4096]{1,0:T(8,128)} %rate_ref.5, f32[256,4096]{1,0:T(8,128)} %shard_map.106.fwd_ref, f32[256,4096]{1,0:T(8,128)} %shard_map.108.back_ref, ...), custom_call_target="tpu_custom_call" | custom-call | flops 115343360 | bytes 28786688 | tf_op jit(solution)/shard_map/pallas_call | solution.py:292
  118.8 1.2 reshape.19
  119.9 1.0 copy.25
  120.9 6.9 %all-to-all-start.2 = ((f32[16,21,256]{2,1,0:T(8,128)}), f32[16,21,256]{2,1,0:T(8,128)S(1)}, u32[]{:S(2)}, u32[]{:S(2)}) async-start(f32[16,21,256]{2,1,0:T(8,128)} %bitcast.12), calls=%async_computation.2 | async-start | bytes 786432 | tf_op jit(solution)/shard_map/all_to_all | solution.py:361
  127.8 0.9 slice.13
  128.7 1.3 collective-permute-start.1
  130.0 8.7 %collective-permute-done.1 = bf16[3,8,4096]{2,1,0:T(8,128)(2,1)S(1)} collective-permute-done((bf16[3,8,4096]{2,1,0:T(8,128)(2,1)S(1)}, bf16[3,8,4096]{2,1,0:T(8,128)(2,1)S(1)}, u32[]{:S(2)}, u32[]{:S(2)}) %collective-permute-start.1) | collective-permute-done | bytes 196640 | tf_op jit(solution)/shard_map/ppermute | solution.py:20
  140.3 0.8 broadcast_in_dim.2
  141.1 7.0 %all-to-all-start.3 = ((f32[16,22,256]{2,1,0:T(8,128)}), f32[16,22,256]{2,1,0:T(8,128)S(1)}, u32[]{:S(2)}, u32[]{:S(2)}) async-start(f32[16,22,256]{2,1,0:T(8,128)} %broadcast_in_dim.2), calls=%async_computation.3 | async-start | bytes 786432 | tf_op jit(solution)/shard_map/all_to_all | solution.py:368
  148.9 13.8 %shard_map.110 = bf16[3,256,4096]{2,1,0:T(8,128)(2,1)} custom-call(bf16[3,256,4096]{2,1,0:T(8,128)(2,1)} %get-tuple-element.30.gm_ref, f32[3,8,4096]{2,1,0:T(8,128)} %convert_element_type.7.rim_ref, f32[3,7,4096]{2,1,0:T(8,128)} %short_ref.3), custom_call_target="tpu_custom_call" | custom-call | flops 44040192 | bytes 13320192 | tf_op jit(solution)/shard_map/pallas_call | solution.py:292
  163.3 3.1 %psum.7 = f32[]{:T(128)} all-reduce(f32[]{:T(128)} %slice_reduce_fusion), channel_id=1, replica_groups=mesh['ctx'=16,'tp'=2] {'tp'}, use_global_device_ids=true, to_apply=%region_3.0 | all-reduce | flops 1 | bytes 8 | tf_op jit(solution)/shard_map/psum | solution.py:375
  167.2 0.9 mul.31
  (15 shorter events, 4.5 us)
Async XLA Ops:
  1.6 18.5 %collective-permute-start = (bf16[3,8,4096]{2,1,0:T(8,128)(2,1)S(1)}, bf16[3,8,4096]{2,1,0:T(8,128)(2,1)S(1)}, u32[]{:S(2)}, u32[]{:S(2)}) collective-permute-start(bf16[3,8,4096]{2,1,0:T(8,128)(2,1)S(1)} %slice.12), channel_id=1, source_target_pairs={{0,2},{2,4},{4,6},{6,8},{8,10},{10,12},{12,14},{14,16},{16,18},{18... | collective-permute-start | bytes 589832 | tf_op jit(solution)/shard_map/ppermute | solution.py:20
  52.0 19.1 %all-to-all-start = ((bf16[16,2,16,256]{3,2,1,0:T(8,128)(2,1)}), bf16[16,2,16,256]{3,2,1,0:T(8,128)(2,1)S(1)}, u32[]{:S(2)}, u32[]{:S(2)}) async-start(bf16[16,2,16,256]{3,2,1,0:T(8,128)(2,1)} %bitcast.14), calls=%async_computation | async-start | bytes 524288 | tf_op jit(solution)/shard_map/all_to_all | solution.py:332
  71.0 0.7 copy-start
  73.6 19.0 %all-to-all-start.1 = ((bf16[16,2,16,256]{3,2,1,0:T(8,128)(2,1)}), bf16[16,2,16,256]{3,2,1,0:T(8,128)(2,1)S(1)}, u32[]{:S(2)}, u32[]{:S(2)}) async-start(bf16[16,2,16,256]{3,2,1,0:T(8,128)(2,1)} %shard_map.107), calls=%async_computation.1 | async-start | bytes 524288 | tf_op jit(solution)/shard_map/all_to_all | solution.py:348
  120.9 18.1 %all-to-all-start.2 = ((f32[16,21,256]{2,1,0:T(8,128)}), f32[16,21,256]{2,1,0:T(8,128)S(1)}, u32[]{:S(2)}, u32[]{:S(2)}) async-start(f32[16,21,256]{2,1,0:T(8,128)} %bitcast.12), calls=%async_computation.2 | async-start | bytes 786432 | tf_op jit(solution)/shard_map/all_to_all | solution.py:361
  128.7 10.0 %collective-permute-start.1 = (bf16[3,8,4096]{2,1,0:T(8,128)(2,1)S(1)}, bf16[3,8,4096]{2,1,0:T(8,128)(2,1)S(1)}, u32[]{:S(2)}, u32[]{:S(2)}) collective-permute-start(bf16[3,8,4096]{2,1,0:T(8,128)(2,1)S(1)} %slice.13), channel_id=1, source_target_pairs={{2,0},{4,2},{6,4},{8,6},{10,8},{12,10},{14,12},{16,14},{18,16},{20... | collective-permute-start | bytes 589832 | tf_op jit(solution)/shard_map/ppermute | solution.py:20
  141.1 21.5 %all-to-all-start.3 = ((f32[16,22,256]{2,1,0:T(8,128)}), f32[16,22,256]{2,1,0:T(8,128)S(1)}, u32[]{:S(2)}, u32[]{:S(2)}) async-start(f32[16,22,256]{2,1,0:T(8,128)} %broadcast_in_dim.2), calls=%async_computation.3 | async-start | bytes 786432 | tf_op jit(solution)/shard_map/all_to_all | solution.py:368

commit v3 on v2

--- a/solution.py
+++ b/solution.py
@@ -88,31 +88,35 @@
 
 def mix_kernel(
     in_ref, rim_ref, cot_ref, short_ref, rate_ref,
-    gated_ref, grad_ref, key_ref, value_ref, state_ref, rowed,
+    gated_ref, grad_ref, key_ref, value_ref, state_ref, ext, rowed,
 ):
     rows, width = cot_ref.shape
     modes = rate_ref.shape[0]
     taps = short_ref.shape[1]
-    part = 32
+    half = (taps + 1) // 2
+    part = 64
     ids = row_ids()
 
     @pl.loop(0, width // LANES)
     def _(chunk):
         lanes = pl.ds(pl.multiple_of(chunk * LANES, LANES), LANES)
+        for i in range(3):
+            ext[i, 0:RIM, :] = jnp.zeros((RIM, LANES), jnp.float32)
+            ext[i, RIM : 2 * RIM, :] = rim_ref[i, :, lanes]
+            ext[i, 2 * RIM : 2 * RIM + rows, :] = in_ref[i, :, lanes].astype(jnp.float32)
         for first in range(0, rows, part):
             mixed = []
             for i in range(3):
-                own = in_ref[i, first : first + part, lanes].astype(jnp.float32)
-                if first > 0:
-                    prior = in_ref[i, first - 16 : first, lanes].astype(jnp.float32)[16 - RIM : 16]
-                else:
-                    prior = rim_ref[i, :, lanes]
-                both = jnp.concatenate([prior, own], axis=0)
-                total = short_ref[i, 0:1, lanes] * own
-                for j in range(1, taps):
-                    moved = pltpu.roll(both, j, 0)[RIM : RIM + part]
-                    total = total + short_ref[i, j : j + 1, lanes] * moved
-                mixed.append(total)
+                near = None
+                far = None
+                for m in range(half):
+                    seen = ext[i, first + RIM - m : first + 2 * RIM - m + part, :]
+                    term = short_ref[i, m : m + 1, lanes] * seen[RIM:]
+                    near = term if near is None else near + term
+                    if half + m < taps:
+                        term = short_ref[i, half + m : half + m + 1, lanes] * seen
+                        far = term if far is None else far + term
+                mixed.append(near + pltpu.roll(far, half, 0)[RIM:])
             here = slice(first, first + part)
             gated_ref[here, lanes] = (mixed[1] * mixed[2]).astype(jnp.bfloat16)
             grad_ref[here, lanes] = (cot_ref[here, lanes].astype(jnp.float32) * mixed[0]).astype(jnp.bfloat16)
@@ -252,28 +256,32 @@
                 short_ref[i, j : j + 1, lanes] = jnp.sum(sums[i][j], axis=0, keepdims=True)
 
 
-def spread_kernel(gm_ref, rim_ref, short_ref, out_ref):
+def spread_kernel(gm_ref, rim_ref, short_ref, out_ref, ext):
     rows, width = gm_ref.shape[1:]
     taps = short_ref.shape[1]
+    half = (taps + 1) // 2
     part = 64
 
     @pl.loop(0, width // LANES)
     def _(chunk):
         lanes = pl.ds(pl.multiple_of(chunk * LANES, LANES), LANES)
+        for i in range(3):
+            ext[i, 0:rows, :] = gm_ref[i, :, lanes].astype(jnp.float32)
+            ext[i, rows : rows + RIM, :] = rim_ref[i, :, lanes]
+            ext[i, rows + RIM : rows + 2 * RIM, :] = jnp.zeros((RIM, LANES), jnp.float32)
         for first in range(0, rows, part):
-            end = first + part
             for i in range(3):
-                own = gm_ref[i, first:end, lanes].astype(jnp.float32)
-                if end < rows:
-                    beyond = gm_ref[i, end : end + 16, lanes].astype(jnp.float32)[0:RIM]
-                else:
-                    beyond = rim_ref[i, :, lanes]
-                both = jnp.concatenate([own, beyond], axis=0)
-                total = short_ref[i, 0:1, lanes] * own
-                for j in range(1, taps):
-                    moved = pltpu.roll(both, part + RIM - j, 0)[0:part]
-                    total = total + short_ref[i, j : j + 1, lanes] * moved
-                out_ref[i, first:end, lanes] = total.astype(jnp.bfloat16)
+                near = None
+                far = None
+                for m in range(half):
+                    seen = ext[i, first + m : first + m + part + RIM, :]
+                    term = short_ref[i, m : m + 1, lanes] * seen[0:part]
+                    near = term if near is None else near + term
+                    if half + m < taps:
+                        term = short_ref[i, half + m : half + m + 1, lanes] * seen
+                        far = term if far is None else far + term
+                total = near + pltpu.roll(far, part + RIM - half, 0)[0:part]
+                out_ref[i, first : first + part, lanes] = total.astype(jnp.bfloat16)
 
 
 def tiled(shape, tile):
@@ -314,6 +322,7 @@
     high, low = split_table(spectral_table(rows))
     tables = [jnp.asarray(high), jnp.asarray(low)]
     turned = [jnp.asarray(np.ascontiguousarray(high.T)), jnp.asarray(np.ascontiguousarray(low.T))]
+    padded_rows = pltpu.VMEM((3, rows + 2 * RIM, LANES), f32)
     ext_rows = pltpu.VMEM((3, rows + RIM, LANES), f32)
 
     rim = passed_along(inputs[:, rows - RIM :, :], "ctx", 1).astype(f32)
@@ -326,7 +335,7 @@
     gated, grad_mixer, key_mix, value_mix, states = over_channels(
         mix_kernel, [inputs, rim, cotangent, short_filter, decay_rate], [],
         [shape((rows, channels), bf16)] * 4 + [shape((2, modes, channels), bf16)],
-        [pltpu.VMEM((2 * modes, LANES), f32)], tile, 110 * rows * channels,
+        [padded_rows, pltpu.VMEM((2 * modes, LANES), f32)], tile, 110 * rows * channels,
     )
     sent = states.reshape(2, modes, ctx_count, narrow).transpose(2, 0, 1, 3)
     arrived = lax.all_to_all(sent, "ctx", split_axis=0, concat_axis=0, tiled=True)
@@ -368,7 +377,7 @@
     packed = lax.all_to_all(packed, "ctx", split_axis=0, concat_axis=0, tiled=True)
     (grad_inputs,) = over_channels(
         spread_kernel, [grad_mix, next_rim, short_filter], [],
-        [shape((3, rows, channels), bf16)], [], tile, 42 * rows * channels,
+        [shape((3, rows, channels), bf16)], [padded_rows], tile, 42 * rows * channels,
     )
     packed, grad_inputs = lax.optimization_barrier((packed, grad_inputs))
     short_sum = packed[:, : 3 * taps].transpose(1, 0, 2).reshape(3, taps, channels)

time: 169 us -> 164 us (0.970)
  Pallas kernels: 108 us -> 102 us
    pallas_call x6, Pallas kernels: 106 us -> 100 us  [over_channels(): pl.pallas_call(kernel, grid=(channels // tile,), in_specs=[tiled(a.shape,...]
  transfers between devices with their start and end apart: 6 -> 6, of which waited for: 2 -> 2; matrix products, arithmetic and copies ran while one was open for 2% -> 2% of each run, Pallas kernels for 31% -> 30%
where the time goes in v3:
time: 164 us; the launch traced here: 162 us
  Pallas kernels  102 us (62%)
  starting transfers between devices  32.8 us (20%)
  local copies, waits for them, and re-layouts  9.57 us (6%)
  waiting for transfers between devices  8.99 us (5%)
  other arithmetic  4.17 us (3%)
  blocking collectives  3.08 us (2%)
    pallas_call x6, Pallas kernels, over_channels(): pl.pallas_call(kernel, grid=(channels // tile,), in_specs=[tiled(a.shape,...  100 us
    ppermute x2, waiting for transfers between devices, passed_along(): return lax.ppermute(shard, axis, pairs)  8.73 us
    all_to_all x1, starting transfers between devices, per_device(): lax.all_to_all(packed, 'ctx', split_axis=0, concat_axis=0, tiled=True)  6.97 us
    all_to_all x1, starting transfers between devices, per_device(): lax.all_to_all(bounds, 'ctx', split_axis=0, concat_axis=0, tiled=True)  6.9 us
    all_to_all x1, starting transfers between devices, per_device(): lax.all_to_all(terms, 'ctx', split_axis=0, concat_axis=0, tiled=True)  6.89 us
    ppermute x2, starting transfers between devices, passed_along(): return lax.ppermute(shard, axis, pairs)  6.15 us
    all_to_all x1, starting transfers between devices, per_device(): lax.all_to_all(sent, 'ctx', split_axis=0, concat_axis=0, tiled=True)  5.93 us
  transfers between devices with their start and end apart: 6, of which 2 were waited for; matrix products, arithmetic and copies ran while one was open for 2% of the time, Pallas kernels for 30%

profile of v3, /device:TPU:0, one launch (start us, length us, event | category | flops | bytes accessed | tf_op | source)
XLA Modules:
  0.0 162.3 jit_solution(476294894308274295)
XLA Ops:
  0.6 0.9 slice.12
  1.6 4.9 %collective-permute-start = (bf16[3,8,4096]{2,1,0:T(8,128)(2,1)S(1)}, bf16[3,8,4096]{2,1,0:T(8,128)(2,1)S(1)}, u32[]{:S(2)}, u32[]{:S(2)}) collective-permute-start(bf16[3,8,4096]{2,1,0:T(8,128)(2,1)S(1)} %slice.12), channel_id=1, source_target_pairs={{0,2},{2,4},{4,6},{6,8},{8,10},{10,12},{12,14},{14,16},{16,18},{18... | collective-permute-start | bytes 589832 | tf_op jit(solution)/shard_map/ppermute | solution.py:20
  6.4 13.7 %shard_map.104.spec_ref = f32[512,4096]{1,0:T(8,128)} custom-call(f32[16,4096]{1,0:T(8,128)} %res_ref.3, f32[16,4096]{1,0:T(8,128)} %rate_ref.5, bf16[512,256]{1,0:T(8,128)(2,1)} %constant.30.clone.high_ref, bf16[512,256]{1,0:T(8,128)(2,1)} %constant.31.clone.low_ref), custom_call_target="tpu_custom_call" | custom-call | flops 3221225472 | bytes 9437184 | tf_op jit(solution)/shard_map/pallas_call | solution.py:300
  20.1 0.8 convert_element_type.6.rim_ref
  20.9 25.7 %shard_map.105 = (bf16[256,4096]{1,0:T(8,128)(2,1)}, bf16[256,4096]{1,0:T(8,128)(2,1)}, bf16[256,4096]{1,0:T(8,128)(2,1)}, bf16[256,4096]{1,0:T(8,128)(2,1)}, bf16[2,16,4096]{2,1,0:T(8,128)(2,1)}) custom-call(bf16[3,256,4096]{2,1,0:T(8,128)(2,1)} %in_ref.3, f32[3,8,4096]{2,1,0:T(8,128)} %convert_element_type.6.rim_ref, bf16[256,4096]{1,0:T(8,128)(2,1)} %cot_ref.3, ...), custom_call_target="tpu_custom_call" | custom-call | flops 115343360 | bytes 18038784 | tf_op jit(solution)/shard_map/pallas_call | solution.py:300
  46.6 1.7 %copy.26 = bf16[2,2,16,8,256]{4,3,1,0,2:T(8,128)(2,1)} copy(bf16[2,2,16,8,256]{4,3,2,1,0:T(8,128)(2,1)} %bitcast.17) | data formatting | bytes 524288 | tf_op jit(solution)/shard_map/reshape | solution.py:340
  48.3 5.9 %all-to-all-start = ((bf16[16,2,16,256]{3,2,1,0:T(8,128)(2,1)}), bf16[16,2,16,256]{3,2,1,0:T(8,128)(2,1)S(1)}, u32[]{:S(2)}, u32[]{:S(2)}) async-start(bf16[16,2,16,256]{3,2,1,0:T(8,128)(2,1)} %bitcast.14), calls=%async_computation | async-start | bytes 524288 | tf_op jit(solution)/shard_map/all_to_all | solution.py:341
  54.2 1.3 multiply_exponential_fusion.step_ref
  55.5 11.8 %shard_map.106.fwd_ref = f32[256,4096]{1,0:T(8,128)} custom-call(bf16[256,4096]{1,0:T(8,128)(2,1)} %get-tuple-element.21.signal_ref, f32[512,4096]{1,0:T(8,128)} %shard_map.104.spec_ref, bf16[512,256]{1,0:T(8,128)(2,1)} %constant.30.clone.high_ref, bf16[512,256]{1,0:T(8,128)(2,1)} %constant.31.clone.low_ref, bf16[256,512]{1,0:T(8,128)(2,1)} %constant.32.clone.hight_ref, ...), custom_call_target="tpu_custom_call" | custom-call | flops 4294967296 | bytes 15728640 | tf_op jit(solution)/shard_map/pallas_call | solution.py:300
  68.1 1.8 %shard_map.107 = bf16[16,2,16,256]{3,2,1,0:T(8,128)(2,1)} custom-call(bf16[16,2,16,256]{3,2,1,0:T(8,128)(2,1)} %copy-done, f32[16,256]{1,0:T(8,128)} %multiply_exponential_fusion.step_ref), custom_call_target="tpu_custom_call" | custom-call | tf_op jit(solution)/shard_map/pallas_call | solution.py:352
  69.9 6.9 %all-to-all-start.1 = ((bf16[16,2,16,256]{3,2,1,0:T(8,128)(2,1)}), bf16[16,2,16,256]{3,2,1,0:T(8,128)(2,1)S(1)}, u32[]{:S(2)}, u32[]{:S(2)}) async-start(bf16[16,2,16,256]{3,2,1,0:T(8,128)(2,1)} %shard_map.107), calls=%async_computation.1 | async-start | bytes 524288 | tf_op jit(solution)/shard_map/all_to_all | solution.py:357
  76.8 12.1 %shard_map.108.back_ref = f32[256,4096]{1,0:T(8,128)} custom-call(bf16[256,4096]{1,0:T(8,128)(2,1)} %get-tuple-element.24.signal_ref, f32[512,4096]{1,0:T(8,128)} %shard_map.104.spec_ref, bf16[512,256]{1,0:T(8,128)(2,1)} %constant.30.clone.high_ref, bf16[512,256]{1,0:T(8,128)(2,1)} %constant.31.clone.low_ref, bf16[256,512]{1,0:T(8,128)(2,1)} %constant.32.clone.hight_ref, ...), custom_call_target="tpu_custom_call" | custom-call | flops 4294967296 | bytes 15728640 | tf_op jit(solution)/shard_map/pallas_call | solution.py:300
  89.7 25.4 %shard_map.109 = (bf16[3,256,4096]{2,1,0:T(8,128)(2,1)}, f32[3,7,4096]{2,1,0:T(8,128)}) custom-call(bf16[2,16,4096]{2,1,0:T(8,128)(2,1)} %bitcast.15, f32[16,4096]{1,0:T(8,128)} %res_ref.3, f32[16,4096]{1,0:T(8,128)} %rate_ref.5, f32[256,4096]{1,0:T(8,128)} %shard_map.106.fwd_ref, f32[256,4096]{1,0:T(8,128)} %shard_map.108.back_ref, ...), custom_call_target="tpu_custom_call" | custom-call | flops 115343360 | bytes 28786688 | tf_op jit(solution)/shard_map/pallas_call | solution.py:300
  115.1 1.2 reshape.19
  116.2 1.0 copy.25
  117.2 6.9 %all-to-all-start.2 = ((f32[16,21,256]{2,1,0:T(8,128)}), f32[16,21,256]{2,1,0:T(8,128)S(1)}, u32[]{:S(2)}, u32[]{:S(2)}) async-start(f32[16,21,256]{2,1,0:T(8,128)} %bitcast.12), calls=%async_computation.2 | async-start | bytes 786432 | tf_op jit(solution)/shard_map/all_to_all | solution.py:370
  124.1 0.9 slice.13
  125.0 1.3 collective-permute-start.1
  126.3 8.7 %collective-permute-done.1 = bf16[3,8,4096]{2,1,0:T(8,128)(2,1)S(1)} collective-permute-done((bf16[3,8,4096]{2,1,0:T(8,128)(2,1)S(1)}, bf16[3,8,4096]{2,1,0:T(8,128)(2,1)S(1)}, u32[]{:S(2)}, u32[]{:S(2)}) %collective-permute-start.1) | collective-permute-done | bytes 196640 | tf_op jit(solution)/shard_map/ppermute | solution.py:20
  136.6 0.8 broadcast_in_dim.2
  137.4 7.0 %all-to-all-start.3 = ((f32[16,22,256]{2,1,0:T(8,128)}), f32[16,22,256]{2,1,0:T(8,128)S(1)}, u32[]{:S(2)}, u32[]{:S(2)}) async-start(f32[16,22,256]{2,1,0:T(8,128)} %broadcast_in_dim.2), calls=%async_computation.3 | async-start | bytes 786432 | tf_op jit(solution)/shard_map/all_to_all | solution.py:377
  145.1 11.8 %shard_map.110 = bf16[3,256,4096]{2,1,0:T(8,128)(2,1)} custom-call(bf16[3,256,4096]{2,1,0:T(8,128)(2,1)} %get-tuple-element.30.gm_ref, f32[3,8,4096]{2,1,0:T(8,128)} %convert_element_type.7.rim_ref, f32[3,7,4096]{2,1,0:T(8,128)} %short_ref.3), custom_call_target="tpu_custom_call" | custom-call | flops 44040192 | bytes 13320192 | tf_op jit(solution)/shard_map/pallas_call | solution.py:300
  157.5 3.1 %psum.7 = f32[]{:T(128)} all-reduce(f32[]{:T(128)} %slice_reduce_fusion), channel_id=1, replica_groups=mesh['ctx'=16,'tp'=2] {'tp'}, use_global_device_ids=true, to_apply=%region_3.0 | all-reduce | flops 1 | bytes 8 | tf_op jit(solution)/shard_map/psum | solution.py:384
  161.5 0.9 mul.31
  (15 shorter events, 4.5 us)
Async XLA Ops:
  1.6 18.5 %collective-permute-start = (bf16[3,8,4096]{2,1,0:T(8,128)(2,1)S(1)}, bf16[3,8,4096]{2,1,0:T(8,128)(2,1)S(1)}, u32[]{:S(2)}, u32[]{:S(2)}) collective-permute-start(bf16[3,8,4096]{2,1,0:T(8,128)(2,1)S(1)} %slice.12), channel_id=1, source_target_pairs={{0,2},{2,4},{4,6},{6,8},{8,10},{10,12},{12,14},{14,16},{16,18},{18... | collective-permute-start | bytes 589832 | tf_op jit(solution)/shard_map/ppermute | solution.py:20
  48.3 19.1 %all-to-all-start = ((bf16[16,2,16,256]{3,2,1,0:T(8,128)(2,1)}), bf16[16,2,16,256]{3,2,1,0:T(8,128)(2,1)S(1)}, u32[]{:S(2)}, u32[]{:S(2)}) async-start(bf16[16,2,16,256]{3,2,1,0:T(8,128)(2,1)} %bitcast.14), calls=%async_computation | async-start | bytes 524288 | tf_op jit(solution)/shard_map/all_to_all | solution.py:341
  67.3 0.7 copy-start
  69.9 19.0 %all-to-all-start.1 = ((bf16[16,2,16,256]{3,2,1,0:T(8,128)(2,1)}), bf16[16,2,16,256]{3,2,1,0:T(8,128)(2,1)S(1)}, u32[]{:S(2)}, u32[]{:S(2)}) async-start(bf16[16,2,16,256]{3,2,1,0:T(8,128)(2,1)} %shard_map.107), calls=%async_computation.1 | async-start | bytes 524288 | tf_op jit(solution)/shard_map/all_to_all | solution.py:357
  117.2 18.1 %all-to-all-start.2 = ((f32[16,21,256]{2,1,0:T(8,128)}), f32[16,21,256]{2,1,0:T(8,128)S(1)}, u32[]{:S(2)}, u32[]{:S(2)}) async-start(f32[16,21,256]{2,1,0:T(8,128)} %bitcast.12), calls=%async_computation.2 | async-start | bytes 786432 | tf_op jit(solution)/shard_map/all_to_all | solution.py:370
  125.0 10.0 %collective-permute-start.1 = (bf16[3,8,4096]{2,1,0:T(8,128)(2,1)S(1)}, bf16[3,8,4096]{2,1,0:T(8,128)(2,1)S(1)}, u32[]{:S(2)}, u32[]{:S(2)}) collective-permute-start(bf16[3,8,4096]{2,1,0:T(8,128)(2,1)S(1)} %slice.13), channel_id=1, source_target_pairs={{2,0},{4,2},{6,4},{8,6},{10,8},{12,10},{14,12},{16,14},{18,16},{20... | collective-permute-start | bytes 589832 | tf_op jit(solution)/shard_map/ppermute | solution.py:20
  137.4 19.5 %all-to-all-start.3 = ((f32[16,22,256]{2,1,0:T(8,128)}), f32[16,22,256]{2,1,0:T(8,128)S(1)}, u32[]{:S(2)}, u32[]{:S(2)}) async-start(f32[16,22,256]{2,1,0:T(8,128)} %broadcast_in_dim.2), calls=%async_computation.3 | async-start | bytes 786432 | tf_op jit(solution)/shard_map/all_to_all | solution.py:377

commit v4 on v3

--- a/solution.py
+++ b/solution.py
@@ -68,7 +68,7 @@
             taps[pl.ds(pl.multiple_of(block * 8, 8), 8), lanes] = total[0]
             return tuple(t * s for t, s in zip(terms, steps))
 
-        lax.fori_loop(0, rows // 8, body, tuple(terms), unroll=4)
+        lax.fori_loop(0, rows // 8, body, tuple(terms), unroll=8)
 
     whole = taps[...]
     main = whole.astype(jnp.bfloat16)
@@ -141,7 +141,7 @@
             return tuple(ends), tuple(starts)
 
         zero = tuple(jnp.zeros((8, LANES), jnp.float32) for _ in range(modes))
-        ends, starts = lax.fori_loop(0, rows // 16, body, (zero, zero), unroll=2)
+        ends, starts = lax.fori_loop(0, rows // 16, body, (zero, zero), unroll=8)
         for n in range(modes):
             rate = jnp.broadcast_to(rate_ref[n : n + 1, lanes], (8, LANES))
             rowed[n : n + 1, :] = jnp.sum(ends[n] * jnp.exp(-rate * (7.0 - ids)), axis=0, keepdims=True)
@@ -231,7 +231,7 @@
                 tuple(t * s for t, s in zip(downs, steps)),
             )
 
-        lax.fori_loop(0, rows // 8, body, (tuple(ups), tuple(downs)), unroll=2)
+        lax.fori_loop(0, rows // 8, body, (tuple(ups), tuple(downs)), unroll=8)
 
         sums = [[None] * taps for _ in range(3)]
         for first in range(0, rows, part):
@@ -315,7 +315,7 @@
     taps = short_filter.shape[1]
     ctx_count = lax.axis_size("ctx")
     narrow = channels // ctx_count
-    tile = math.gcd(channels, 512)
+    tile = math.gcd(channels, 1024)
     f32 = jnp.float32
     bf16 = jnp.bfloat16
     shape = jax.ShapeDtypeStruct

time: 164 us -> 158 us (0.963)
  Pallas kernels: 102 us -> 97.1 us
    pallas_call x6, Pallas kernels: 100 us -> 95.3 us  [over_channels(): pl.pallas_call(kernel, grid=(channels // tile,), in_specs=[tiled(a.shape,...]
  transfers between devices with their start and end apart: 6 -> 6, of which waited for: 2 -> 2; matrix products, arithmetic and copies ran while one was open for 2% -> 2% of each run, Pallas kernels for 30% -> 28%
where the time goes in v4:
time: 158 us; the launch traced here: 157 us
  Pallas kernels  97.1 us (61%)
  starting transfers between devices  32.8 us (21%)
  local copies, waits for them, and re-layouts  9.57 us (6%)
  waiting for transfers between devices  9.01 us (6%)
  other arithmetic  4.17 us (3%)
  blocking collectives  3.08 us (2%)
    pallas_call x6, Pallas kernels, over_channels(): pl.pallas_call(kernel, grid=(channels // tile,), in_specs=[tiled(a.shape,...  95.3 us
    ppermute x2, waiting for transfers between devices, passed_along(): return lax.ppermute(shard, axis, pairs)  8.75 us
    all_to_all x1, starting transfers between devices, per_device(): lax.all_to_all(packed, 'ctx', split_axis=0, concat_axis=0, tiled=True)  6.97 us
    all_to_all x1, starting transfers between devices, per_device(): lax.all_to_all(terms, 'ctx', split_axis=0, concat_axis=0, tiled=True)  6.89 us
    all_to_all x1, starting transfers between devices, per_device(): lax.all_to_all(bounds, 'ctx', split_axis=0, concat_axis=0, tiled=True)  6.89 us
    ppermute x2, starting transfers between devices, passed_along(): return lax.ppermute(shard, axis, pairs)  6.15 us
    all_to_all x1, starting transfers between devices, per_device(): lax.all_to_all(sent, 'ctx', split_axis=0, concat_axis=0, tiled=True)  5.93 us
  transfers between devices with their start and end apart: 6, of which 2 were waited for; matrix products, arithmetic and copies ran while one was open for 2% of the time, Pallas kernels for 28%

profile of v4, /device:TPU:0, one launch (start us, length us, event | category | flops | bytes accessed | tf_op | source)
XLA Modules:
  0.0 157.3 jit_solution(13972882567315556619)
XLA Ops:
  0.6 0.9 slice.12
  1.6 4.9 %collective-permute-start = (bf16[3,8,4096]{2,1,0:T(8,128)(2,1)S(1)}, bf16[3,8,4096]{2,1,0:T(8,128)(2,1)S(1)}, u32[]{:S(2)}, u32[]{:S(2)}) collective-permute-start(bf16[3,8,4096]{2,1,0:T(8,128)(2,1)S(1)} %slice.12), channel_id=1, source_target_pairs={{0,2},{2,4},{4,6},{6,8},{8,10},{10,12},{12,14},{14,16},{16,18},{18... | collective-permute-start | bytes 589832 | tf_op jit(solution)/shard_map/ppermute | solution.py:20
  6.4 12.6 %shard_map.104.spec_ref = f32[512,4096]{1,0:T(8,128)} custom-call(f32[16,4096]{1,0:T(8,128)} %res_ref.3, f32[16,4096]{1,0:T(8,128)} %rate_ref.5, bf16[512,256]{1,0:T(8,128)(2,1)} %constant.30.clone.high_ref, bf16[512,256]{1,0:T(8,128)(2,1)} %constant.31.clone.low_ref), custom_call_target="tpu_custom_call" | custom-call | flops 3221225472 | bytes 9437184 | tf_op jit(solution)/shard_map/pallas_call | solution.py:300
  19.1 0.8 convert_element_type.6.rim_ref
  19.8 25.5 %shard_map.105 = (bf16[256,4096]{1,0:T(8,128)(2,1)}, bf16[256,4096]{1,0:T(8,128)(2,1)}, bf16[256,4096]{1,0:T(8,128)(2,1)}, bf16[256,4096]{1,0:T(8,128)(2,1)}, bf16[2,16,4096]{2,1,0:T(8,128)(2,1)}) custom-call(bf16[3,256,4096]{2,1,0:T(8,128)(2,1)} %in_ref.3, f32[3,8,4096]{2,1,0:T(8,128)} %convert_element_type.6.rim_ref, bf16[256,4096]{1,0:T(8,128)(2,1)} %cot_ref.3, ...), custom_call_target="tpu_custom_call" | custom-call | flops 115343360 | bytes 18038784 | tf_op jit(solution)/shard_map/pallas_call | solution.py:300
  45.4 1.7 %copy.26 = bf16[2,2,16,8,256]{4,3,1,0,2:T(8,128)(2,1)} copy(bf16[2,2,16,8,256]{4,3,2,1,0:T(8,128)(2,1)} %bitcast.17) | data formatting | bytes 524288 | tf_op jit(solution)/shard_map/reshape | solution.py:340
  47.1 5.9 %all-to-all-start = ((bf16[16,2,16,256]{3,2,1,0:T(8,128)(2,1)}), bf16[16,2,16,256]{3,2,1,0:T(8,128)(2,1)S(1)}, u32[]{:S(2)}, u32[]{:S(2)}) async-start(bf16[16,2,16,256]{3,2,1,0:T(8,128)(2,1)} %bitcast.14), calls=%async_computation | async-start | bytes 524288 | tf_op jit(solution)/shard_map/all_to_all | solution.py:341
  53.0 1.3 multiply_exponential_fusion.step_ref
  54.3 9.6 %shard_map.106.fwd_ref = f32[256,4096]{1,0:T(8,128)} custom-call(bf16[256,4096]{1,0:T(8,128)(2,1)} %get-tuple-element.21.signal_ref, f32[512,4096]{1,0:T(8,128)} %shard_map.104.spec_ref, bf16[512,256]{1,0:T(8,128)(2,1)} %constant.30.clone.high_ref, bf16[512,256]{1,0:T(8,128)(2,1)} %constant.31.clone.low_ref, bf16[256,512]{1,0:T(8,128)(2,1)} %constant.32.clone.hight_ref, ...), custom_call_target="tpu_custom_call" | custom-call | flops 4294967296 | bytes 15728640 | tf_op jit(solution)/shard_map/pallas_call | solution.py:300
  64.6 1.8 %shard_map.107 = bf16[16,2,16,256]{3,2,1,0:T(8,128)(2,1)} custom-call(bf16[16,2,16,256]{3,2,1,0:T(8,128)(2,1)} %copy-done, f32[16,256]{1,0:T(8,128)} %multiply_exponential_fusion.step_ref), custom_call_target="tpu_custom_call" | custom-call | tf_op jit(solution)/shard_map/pallas_call | solution.py:352
  66.5 6.9 %all-to-all-start.1 = ((bf16[16,2,16,256]{3,2,1,0:T(8,128)(2,1)}), bf16[16,2,16,256]{3,2,1,0:T(8,128)(2,1)S(1)}, u32[]{:S(2)}, u32[]{:S(2)}) async-start(bf16[16,2,16,256]{3,2,1,0:T(8,128)(2,1)} %shard_map.107), calls=%async_computation.1 | async-start | bytes 524288 | tf_op jit(solution)/shard_map/all_to_all | solution.py:357
  73.4 9.8 %shard_map.108.back_ref = f32[256,4096]{1,0:T(8,128)} custom-call(bf16[256,4096]{1,0:T(8,128)(2,1)} %get-tuple-element.24.signal_ref, f32[512,4096]{1,0:T(8,128)} %shard_map.104.spec_ref, bf16[512,256]{1,0:T(8,128)(2,1)} %constant.30.clone.high_ref, bf16[512,256]{1,0:T(8,128)(2,1)} %constant.31.clone.low_ref, bf16[256,512]{1,0:T(8,128)(2,1)} %constant.32.clone.hight_ref, ...), custom_call_target="tpu_custom_call" | custom-call | flops 4294967296 | bytes 15728640 | tf_op jit(solution)/shard_map/pallas_call | solution.py:300
  83.9 26.1 %shard_map.109 = (bf16[3,256,4096]{2,1,0:T(8,128)(2,1)}, f32[3,7,4096]{2,1,0:T(8,128)}) custom-call(bf16[2,16,4096]{2,1,0:T(8,128)(2,1)} %bitcast.15, f32[16,4096]{1,0:T(8,128)} %res_ref.3, f32[16,4096]{1,0:T(8,128)} %rate_ref.5, f32[256,4096]{1,0:T(8,128)} %shard_map.106.fwd_ref, f32[256,4096]{1,0:T(8,128)} %shard_map.108.back_ref, ...), custom_call_target="tpu_custom_call" | custom-call | flops 115343360 | bytes 28786688 | tf_op jit(solution)/shard_map/pallas_call | solution.py:300
  110.0 1.2 reshape.19
  111.2 1.0 copy.25
  112.1 6.9 %all-to-all-start.2 = ((f32[16,21,256]{2,1,0:T(8,128)}), f32[16,21,256]{2,1,0:T(8,128)S(1)}, u32[]{:S(2)}, u32[]{:S(2)}) async-start(f32[16,21,256]{2,1,0:T(8,128)} %bitcast.12), calls=%async_computation.2 | async-start | bytes 786432 | tf_op jit(solution)/shard_map/all_to_all | solution.py:370
  119.0 0.9 slice.13
  120.0 1.3 collective-permute-start.1
  121.3 8.7 %collective-permute-done.1 = bf16[3,8,4096]{2,1,0:T(8,128)(2,1)S(1)} collective-permute-done((bf16[3,8,4096]{2,1,0:T(8,128)(2,1)S(1)}, bf16[3,8,4096]{2,1,0:T(8,128)(2,1)S(1)}, u32[]{:S(2)}, u32[]{:S(2)}) %collective-permute-start.1) | collective-permute-done | bytes 196640 | tf_op jit(solution)/shard_map/ppermute | solution.py:20
  131.6 0.8 broadcast_in_dim.2
  132.3 7.0 %all-to-all-start.3 = ((f32[16,22,256]{2,1,0:T(8,128)}), f32[16,22,256]{2,1,0:T(8,128)S(1)}, u32[]{:S(2)}, u32[]{:S(2)}) async-start(f32[16,22,256]{2,1,0:T(8,128)} %broadcast_in_dim.2), calls=%async_computation.3 | async-start | bytes 786432 | tf_op jit(solution)/shard_map/all_to_all | solution.py:377
  140.1 11.7 %shard_map.110 = bf16[3,256,4096]{2,1,0:T(8,128)(2,1)} custom-call(bf16[3,256,4096]{2,1,0:T(8,128)(2,1)} %get-tuple-element.30.gm_ref, f32[3,8,4096]{2,1,0:T(8,128)} %convert_element_type.7.rim_ref, f32[3,7,4096]{2,1,0:T(8,128)} %short_ref.3), custom_call_target="tpu_custom_call" | custom-call | flops 44040192 | bytes 13320192 | tf_op jit(solution)/shard_map/pallas_call | solution.py:300
  152.4 3.1 %psum.7 = f32[]{:T(128)} all-reduce(f32[]{:T(128)} %slice_reduce_fusion), channel_id=1, replica_groups=mesh['ctx'=16,'tp'=2] {'tp'}, use_global_device_ids=true, to_apply=%region_3.0 | all-reduce | flops 1 | bytes 8 | tf_op jit(solution)/shard_map/psum | solution.py:384
  156.4 0.9 mul.31
  (15 shorter events, 4.5 us)
Async XLA Ops:
  1.6 17.5 %collective-permute-start = (bf16[3,8,4096]{2,1,0:T(8,128)(2,1)S(1)}, bf16[3,8,4096]{2,1,0:T(8,128)(2,1)S(1)}, u32[]{:S(2)}, u32[]{:S(2)}) collective-permute-start(bf16[3,8,4096]{2,1,0:T(8,128)(2,1)S(1)} %slice.12), channel_id=1, source_target_pairs={{0,2},{2,4},{4,6},{6,8},{8,10},{10,12},{12,14},{14,16},{16,18},{18... | collective-permute-start | bytes 589832 | tf_op jit(solution)/shard_map/ppermute | solution.py:20
  47.1 16.8 %all-to-all-start = ((bf16[16,2,16,256]{3,2,1,0:T(8,128)(2,1)}), bf16[16,2,16,256]{3,2,1,0:T(8,128)(2,1)S(1)}, u32[]{:S(2)}, u32[]{:S(2)}) async-start(bf16[16,2,16,256]{3,2,1,0:T(8,128)(2,1)} %bitcast.14), calls=%async_computation | async-start | bytes 524288 | tf_op jit(solution)/shard_map/all_to_all | solution.py:341
  63.9 0.7 copy-start
  66.5 16.7 %all-to-all-start.1 = ((bf16[16,2,16,256]{3,2,1,0:T(8,128)(2,1)}), bf16[16,2,16,256]{3,2,1,0:T(8,128)(2,1)S(1)}, u32[]{:S(2)}, u32[]{:S(2)}) async-start(bf16[16,2,16,256]{3,2,1,0:T(8,128)(2,1)} %shard_map.107), calls=%async_computation.1 | async-start | bytes 524288 | tf_op jit(solution)/shard_map/all_to_all | solution.py:357
  112.1 18.1 %all-to-all-start.2 = ((f32[16,21,256]{2,1,0:T(8,128)}), f32[16,21,256]{2,1,0:T(8,128)S(1)}, u32[]{:S(2)}, u32[]{:S(2)}) async-start(f32[16,21,256]{2,1,0:T(8,128)} %bitcast.12), calls=%async_computation.2 | async-start | bytes 786432 | tf_op jit(solution)/shard_map/all_to_all | solution.py:370
  120.0 10.0 %collective-permute-start.1 = (bf16[3,8,4096]{2,1,0:T(8,128)(2,1)S(1)}, bf16[3,8,4096]{2,1,0:T(8,128)(2,1)S(1)}, u32[]{:S(2)}, u32[]{:S(2)}) collective-permute-start(bf16[3,8,4096]{2,1,0:T(8,128)(2,1)S(1)} %slice.13), channel_id=1, source_target_pairs={{2,0},{4,2},{6,4},{8,6},{10,8},{12,10},{14,12},{16,14},{18,16},{20... | collective-permute-start | bytes 589832 | tf_op jit(solution)/shard_map/ppermute | solution.py:20
  132.3 19.5 %all-to-all-start.3 = ((f32[16,22,256]{2,1,0:T(8,128)}), f32[16,22,256]{2,1,0:T(8,128)S(1)}, u32[]{:S(2)}, u32[]{:S(2)}) async-start(f32[16,22,256]{2,1,0:T(8,128)} %broadcast_in_dim.2), calls=%async_computation.3 | async-start | bytes 786432 | tf_op jit(solution)/shard_map/all_to_all | solution.py:377
